TPU v7x, 128 devices: a whole 4x4x4 slice. The times are simulated.
128 devices in a mesh: section: 8 (over z_hi, y), slab: 16 (over z_lo, x, core).
Axes of the slice: x: 4, y: 4, z: 4 (z_hi: 2, z_lo: 2; z = z_hi * 2 + z_lo), core: 2. Of those that a mesh axis runs over, the one named last changes fastest.
Arguments:
- features_in: bfloat16 [2, 256, 16, 2, 64], P(None, None, 'slab'), may hold values from -6 to 6
- labels: int32 [2, 16, 2, 64], P(None, 'slab'), may hold values from 0 to 5
- offsets: int32 [3, 3], replicated, may hold values from -1 to 1, as said below
- conv_weight: bfloat16 [8, 3, 3, 3, 256, 256], P('section'), may hold values from -0.078125 to 0.078125
- branch_weight: bfloat16 [8, 256, 256], P('section'), may hold values from -0.375 to 0.375
- head_weight: bfloat16 [256, 3], replicated, may hold values from -0.375 to 0.375
Outputs:
- loss: float32 [], replicated
- grad_conv: float32 [8, 3, 3, 3, 256, 256], P('section')
- grad_branch: float32 [8, 256, 256], P('section')
- grad_head: float32 [256, 3], replicated
Inputs may be any that keep to these rules, and one draw needn't show every extreme that they name: Row j of the offsets has a nonzero entry j.
All inputs are finite; a program needn't handle non-finite values.
Results may differ from a plain program's by a relative error of at most 0.0023.
Values may be sent and summed in bfloat16 or wider, within the bound.
A program may use at most 64 MiB of HBM per device.

v0:
```python
import jax
import jax.numpy as jnp
from jax import lax
from jax.sharding import PartitionSpec as P

loss_scale = 1024.0


def extended(block, sides, width):
    for axis, dim in sides:
        count = lax.axis_size(axis)
        forward = [(i, i + 1) for i in range(count - 1)]
        backward = [(target, source) for source, target in forward]
        low = lax.ppermute(
            lax.slice_in_dim(block, block.shape[dim] - width, None, axis=dim), axis, forward
        )
        high = lax.ppermute(lax.slice_in_dim(block, 0, width, axis=dim), axis, backward)
        block = jnp.concatenate([low, block, high], axis=dim)
    return block


def from_behind(x, axis, by):
    peers = lax.axis_size(axis)
    pairs = [(i, i + by) for i in range(peers) if 0 <= i + by < peers]
    return lax.ppermute(x, axis, pairs)


def partner(block, axis, apart):
    count = lax.axis_size(axis)
    route = []
    for low in range(count):
        high = low | 1 << apart
        if high != low and high < count:
            route += [(low, high), (high, low)]
    return lax.ppermute(block, axis, route)


def conv_local(padded, kernel):
    result = lax.conv_general_dilated(
        padded[None],
        kernel,
        (1, 1, 1),
        ((0, 0), (1, 1), (1, 1)),
        dimension_numbers=("NCDHW", "DHWIO", "NCDHW"),
        preferred_element_type=jnp.float32,
    )
    return result[0]


def weight_grad(padded, cotangent):
    result = lax.conv_general_dilated(
        padded[:, None],
        cotangent[:, None],
        (1, 1, 1),
        ((0, 0), (1, 1), (1, 1)),
        dimension_numbers=("NCDHW", "OIDHW", "NCDHW"),
        preferred_element_type=jnp.float32,
    )
    return jnp.transpose(result, (2, 3, 4, 0, 1))


def silu_slope(preact):
    logistic = jax.nn.sigmoid(preact)
    return logistic * (1.0 + preact * (1.0 - logistic))


def with_faces(volume):
    return extended(volume, (("slab", 1),), 1)


def pass_along(volume, hops):
    return from_behind(volume, "section", hops)


def mirror(volume):
    section_count = lax.axis_size("section")
    bit_count = section_count.bit_length() - 1
    bit_order = list(range(bit_count))
    for bit_number in bit_order:
        volume = partner(volume, "section", bit_number)
    return volume


def take_slot(buffer, slot_id):
    return lax.dynamic_index_in_dim(buffer, slot_id, 0, keepdims=False)


def put_slot(buffer, slot_id, value, active):
    previous = take_slot(buffer, slot_id)
    return lax.dynamic_update_index_in_dim(buffer, jnp.where(active, value, previous), slot_id, 0)


def body(features_in, labels, offsets, conv_weight, branch_weight, head_weight):
    sections = lax.axis_size("section")
    half = sections // 2
    section = lax.axis_index("section")
    encoder = section < half
    final_section = section == sections - 1
    micro = features_in.shape[0]
    moments = micro + sections - 1
    kernel = conv_weight[0]
    flipped = jnp.swapaxes(jnp.flip(kernel, (0, 1, 2)), 3, 4)
    mixing = branch_weight[0]
    act_shape = features_in.shape[1:]
    depth = act_shape[1]
    padded_shape = (act_shape[0], depth + 2, act_shape[2], act_shape[3])
    zero_act = jnp.zeros(act_shape, jnp.bfloat16)
    pads = jnp.zeros((micro,) + padded_shape, jnp.bfloat16)
    branches = jnp.zeros((micro,) + act_shape, jnp.bfloat16)
    outputs = jnp.zeros((micro,) + act_shape, jnp.bfloat16)
    skips = jnp.zeros((micro,) + act_shape, jnp.bfloat16)
    preacts = jnp.zeros((micro,) + act_shape, jnp.float32)

    def forward_step(moment, loop_state):
        incoming, skips, pads, branches, preacts, outputs = loop_state
        micro_id = moment - section
        active = (micro_id >= 0) & (micro_id < micro)
        slot_id = jnp.clip(micro_id, 0, micro - 1)
        current = jnp.where(section == 0, take_slot(features_in, slot_id), incoming)
        branch = jnp.where(encoder, current, take_slot(skips, slot_id))
        padded = with_faces(current)
        preact = conv_local(padded, kernel) + jnp.einsum(
            "io,izyx->ozyx", mixing, branch, preferred_element_type=jnp.float32
        )
        output = jax.nn.silu(preact).astype(jnp.bfloat16)
        pads = put_slot(pads, slot_id, padded, active)
        branches = put_slot(branches, slot_id, branch, active)
        outputs = put_slot(outputs, slot_id, output, active)
        preacts = put_slot(preacts, slot_id, preact, active)
        incoming = pass_along(output, 1)
        arrived = mirror(output)
        partner_id = moment - (sections - 1 - section)
        landing = jnp.logical_not(encoder) & (partner_id >= 0) & (partner_id < micro)
        skips = put_slot(skips, jnp.clip(partner_id, 0, micro - 1), arrived, landing)
        return (incoming, skips, pads, branches, preacts, outputs)

    loop_state = (zero_act, skips, pads, branches, preacts, outputs)
    loop_state = lax.fori_loop(0, moments, forward_step, loop_state)
    skips, pads, branches, preacts, outputs = (
        loop_state[1],
        loop_state[2],
        loop_state[3],
        loop_state[4],
        loop_state[5],
    )
    count = micro * offsets.shape[0] * depth * act_shape[2] * act_shape[3] * lax.axis_size("slab")
    logits = jnp.einsum("co,mczyx->mozyx", head_weight, outputs, preferred_element_type=jnp.float32)
    label_pad = extended(labels, (("slab", 1),), 1)
    label_pad = jnp.pad(label_pad, ((0, 0), (0, 0), (1, 1), (1, 1)))
    zero_index = jnp.zeros((), jnp.int32)
    target_maps = []
    for channel in range(offsets.shape[0]):
        neighbor = lax.dynamic_slice(
            label_pad,
            (zero_index, 1 + offsets[channel, 0], 1 + offsets[channel, 1], 1 + offsets[channel, 2]),
            labels.shape,
        )
        same = (neighbor == labels) & (labels != 0)
        target_maps.append(jnp.where(same, 1.0, 0.0).astype(jnp.float32))
    targets = jnp.stack(target_maps, axis=1)
    loss_part = jnp.where(final_section, jnp.sum(jax.nn.softplus(logits) - targets * logits), 0.0)
    logit_grad = (loss_scale * (jax.nn.sigmoid(logits) - targets) / count).astype(jnp.bfloat16)
    head_part = jnp.einsum(
        "mczyx,mozyx->co", outputs, logit_grad, preferred_element_type=jnp.float32
    )
    head_part = jnp.where(final_section, head_part, 0.0)
    loss_sum, grad_head = lax.psum((loss_part, head_part), ("section", "slab"))
    head_cotangent = jnp.einsum(
        "co,mozyx->mczyx", head_weight, logit_grad, preferred_element_type=jnp.float32
    )

    def backward_step(moment, loop_state):
        incoming, skip_grads, grad_kernel, grad_mixing = loop_state
        micro_id = moment - (sections - 1 - section)
        active = (micro_id >= 0) & (micro_id < micro)
        slot_id = jnp.clip(micro_id, 0, micro - 1)
        from_skip = jnp.where(encoder, take_slot(skip_grads, slot_id).astype(jnp.float32), 0.0)
        upstream = jnp.where(
            final_section,
            take_slot(head_cotangent, slot_id),
            incoming.astype(jnp.float32) + from_skip,
        )
        padded = take_slot(pads, slot_id)
        branch = take_slot(branches, slot_id)
        preact = take_slot(preacts, slot_id)
        pre_grad = (upstream * silu_slope(preact)).astype(jnp.bfloat16)
        grad_kernel = grad_kernel + jnp.where(active, weight_grad(padded, pre_grad), 0.0)
        grad_mixing = grad_mixing + jnp.where(
            active,
            jnp.einsum("izyx,ozyx->io", branch, pre_grad, preferred_element_type=jnp.float32),
            0.0,
        )
        branch_grad = jnp.einsum(
            "io,ozyx->izyx", mixing, pre_grad, preferred_element_type=jnp.float32
        )
        input_grad = conv_local(with_faces(pre_grad), flipped)
        sent_down = jnp.where(encoder, input_grad + branch_grad, input_grad).astype(jnp.bfloat16)
        incoming = pass_along(sent_down, -1)
        arrived = mirror(branch_grad.astype(jnp.bfloat16))
        partner_id = moment - section
        landing = encoder & (partner_id >= 0) & (partner_id < micro)
        skip_grads = put_slot(skip_grads, jnp.clip(partner_id, 0, micro - 1), arrived, landing)
        return (incoming, skip_grads, grad_kernel, grad_mixing)

    loop_state = (
        zero_act,
        jnp.zeros((micro,) + act_shape, jnp.bfloat16),
        jnp.zeros(kernel.shape, jnp.float32),
        jnp.zeros(mixing.shape, jnp.float32),
    )
    loop_state = lax.fori_loop(0, moments, backward_step, loop_state)
    grad_kernel, grad_mixing = lax.psum((loop_state[2], loop_state[3]), "slab")
    return (loss_sum / count, grad_kernel[None], grad_mixing[None], grad_head)


def solution(mesh):
    placed = (
        P(None, None, "slab", None, None),
        P(None, "slab", None, None),
        P(),
        P("section", None, None, None, None, None),
        P("section", None, None),
        P(),
    )
    return jax.shard_map(
        body,
        mesh=mesh,
        in_specs=placed,
        out_specs=(P(), P("section", None, None, None, None, None), P("section", None, None), P()),
        check_vma=False,
    )
```

profile of v0, /device:TPU:1, one launch (start us, length us, event | category | flops | bytes accessed | tf_op | source)
XLA Modules:
  0.0 850.7 jit_solution(12448344522990656003)
XLA Ops:
  26.8 6.2 copy.35
  43.4 290.9 %while.45 = (s32[]{:T(128)}, bf16[256,1,2,64]{0,3,2,1:T(8,128)(2,1)}, bf16[2,256,1,2,64]{1,4,3,2,0:T(8,128)(2,1)}, bf16[2,256,3,2,64]{1,4,3,2,0:T(8,128)(2,1)}, ...) while((s32[]{:T(128)}, ...), condition=%wide.region_1.2_spmd, body=%wide.region_0.1_spmd.sunk | while | flops 358838272 | bytes 16664424 | solution.py:138
  236.6 6.4 collective-permute-start.1
  269.6 6.3 collective-permute-start.1
  302.6 7.6 collective-permute-start.1
  336.9 345.4 %while.46 = (s32[]{:T(128)}, bf16[256,1,2,64]{0,3,2,1:T(8,128)(2,1)S(1)}, bf16[2,256,1,2,64]{1,4,3,2,0:T(8,128)(2,1)S(1)}, f32[3,3,3,256,256]{4,3,2,1,0:T(8,128)...) while((s32[]{:T(128)}, ...), condition=%wide.region_5.6_spmd.clone, body=%wide.region_4.5_spmd.clone.sunk | while | flops 679309312 | bytes 27671296 | solution.py:211
  338.0 6.5 collective-permute-start.7
  370.5 5.8 collective-permute-start.7
  387.4 8.7 %select_add_fusion.2 = f32[3,3,3,256,256]{4,3,2,1,0:T(8,128)} fusion(f32[3,3,3,256,256]{4,3,2,1,0:T(8,128)} %get-tuple-element.1035, pred[]{:T(512)S(6)} %compare.26, pred[]{:T(512)S(6)} %and.78, bf16[256,1,3,2,64]{0,4,3,2,1:T(8,128)(2,1)S(1)} %dynamic-slice_bitcast_fusion.2, bf16[256,1,1,2,64]{0,4,3,2,1:T(8,128)(2,1)S(1)} %bitcast.310), kind=kOutput, calls=%fused_computation.37.clone.1 | convolution fusion | flops 304152576 | bytes 14417922 | tf_op jit(solution)/shard_map/while/body/eval_jaxpr/transpose | solution.py:59
  424.7 8.7 %select_add_fusion.2 = f32[3,3,3,256,256]{4,3,2,1,0:T(8,128)} fusion(f32[3,3,3,256,256]{4,3,2,1,0:T(8,128)} %get-tuple-element.1035, pred[]{:T(512)S(6)} %compare.26, pred[]{:T(512)S(6)} %and.78, bf16[256,1,3,2,64]{0,4,3,2,1:T(8,128)(2,1)S(1)} %dynamic-slice_bitcast_fusion.2, bf16[256,1,1,2,64]{0,4,3,2,1:T(8,128)(2,1)S(1)} %bitcast.310), kind=kOutput, calls=%fused_computation.37.clone.1 | convolution fusion | flops 304152576 | bytes 14417922 | tf_op jit(solution)/shard_map/while/body/eval_jaxpr/transpose | solution.py:59
  433.4 6.2 collective-permute-start.10
  447.9 6.2 collective-permute-start.7
  463.3 8.7 %select_add_fusion.2 = f32[3,3,3,256,256]{4,3,2,1,0:T(8,128)} fusion(f32[3,3,3,256,256]{4,3,2,1,0:T(8,128)} %get-tuple-element.1035, pred[]{:T(512)S(6)} %compare.26, pred[]{:T(512)S(6)} %and.78, bf16[256,1,3,2,64]{0,4,3,2,1:T(8,128)(2,1)S(1)} %dynamic-slice_bitcast_fusion.2, bf16[256,1,1,2,64]{0,4,3,2,1:T(8,128)(2,1)S(1)} %bitcast.310), kind=kOutput, calls=%fused_computation.37.clone.1 | convolution fusion | flops 304152576 | bytes 14417922 | tf_op jit(solution)/shard_map/while/body/eval_jaxpr/transpose | solution.py:59
  472.0 7.1 collective-permute-start.10
  486.8 6.5 collective-permute-start.7
  502.5 8.7 %select_add_fusion.2 = f32[3,3,3,256,256]{4,3,2,1,0:T(8,128)} fusion(f32[3,3,3,256,256]{4,3,2,1,0:T(8,128)} %get-tuple-element.1035, pred[]{:T(512)S(6)} %compare.26, pred[]{:T(512)S(6)} %and.78, bf16[256,1,3,2,64]{0,4,3,2,1:T(8,128)(2,1)S(1)} %dynamic-slice_bitcast_fusion.2, bf16[256,1,1,2,64]{0,4,3,2,1:T(8,128)(2,1)S(1)} %bitcast.310), kind=kOutput, calls=%fused_computation.37.clone.1 | convolution fusion | flops 304152576 | bytes 14417922 | tf_op jit(solution)/shard_map/while/body/eval_jaxpr/transpose | solution.py:59
  511.2 7.1 collective-permute-start.10
  526.0 6.9 collective-permute-start.7
  542.1 8.7 %select_add_fusion.2 = f32[3,3,3,256,256]{4,3,2,1,0:T(8,128)} fusion(f32[3,3,3,256,256]{4,3,2,1,0:T(8,128)} %get-tuple-element.1035, pred[]{:T(512)S(6)} %compare.26, pred[]{:T(512)S(6)} %and.78, bf16[256,1,3,2,64]{0,4,3,2,1:T(8,128)(2,1)S(1)} %dynamic-slice_bitcast_fusion.2, bf16[256,1,1,2,64]{0,4,3,2,1:T(8,128)(2,1)S(1)} %bitcast.310), kind=kOutput, calls=%fused_computation.37.clone.1 | convolution fusion | flops 304152576 | bytes 14417922 | tf_op jit(solution)/shard_map/while/body/eval_jaxpr/transpose | solution.py:59
  550.8 7.1 collective-permute-start.10
  565.5 6.5 collective-permute-start.7
  581.2 8.7 %select_add_fusion.2 = f32[3,3,3,256,256]{4,3,2,1,0:T(8,128)} fusion(f32[3,3,3,256,256]{4,3,2,1,0:T(8,128)} %get-tuple-element.1035, pred[]{:T(512)S(6)} %compare.26, pred[]{:T(512)S(6)} %and.78, bf16[256,1,3,2,64]{0,4,3,2,1:T(8,128)(2,1)S(1)} %dynamic-slice_bitcast_fusion.2, bf16[256,1,1,2,64]{0,4,3,2,1:T(8,128)(2,1)S(1)} %bitcast.310), kind=kOutput, calls=%fused_computation.37.clone.1 | convolution fusion | flops 304152576 | bytes 14417922 | tf_op jit(solution)/shard_map/while/body/eval_jaxpr/transpose | solution.py:59
  589.8 7.1 collective-permute-start.10
  604.6 6.9 collective-permute-start.7
  620.8 8.7 %select_add_fusion.2 = f32[3,3,3,256,256]{4,3,2,1,0:T(8,128)} fusion(f32[3,3,3,256,256]{4,3,2,1,0:T(8,128)} %get-tuple-element.1035, pred[]{:T(512)S(6)} %compare.26, pred[]{:T(512)S(6)} %and.78, bf16[256,1,3,2,64]{0,4,3,2,1:T(8,128)(2,1)S(1)} %dynamic-slice_bitcast_fusion.2, bf16[256,1,1,2,64]{0,4,3,2,1:T(8,128)(2,1)S(1)} %bitcast.310), kind=kOutput, calls=%fused_computation.37.clone.1 | convolution fusion | flops 304152576 | bytes 14417922 | tf_op jit(solution)/shard_map/while/body/eval_jaxpr/transpose | solution.py:59
  629.4 7.1 collective-permute-start.10
  644.2 6.5 collective-permute-start.7
  659.8 8.7 %select_add_fusion.2 = f32[3,3,3,256,256]{4,3,2,1,0:T(8,128)} fusion(f32[3,3,3,256,256]{4,3,2,1,0:T(8,128)} %get-tuple-element.1035, pred[]{:T(512)S(6)} %compare.26, pred[]{:T(512)S(6)} %and.78, bf16[256,1,3,2,64]{0,4,3,2,1:T(8,128)(2,1)S(1)} %dynamic-slice_bitcast_fusion.2, bf16[256,1,1,2,64]{0,4,3,2,1:T(8,128)(2,1)S(1)} %bitcast.310), kind=kOutput, calls=%fused_computation.37.clone.1 | convolution fusion | flops 304152576 | bytes 14417922 | tf_op jit(solution)/shard_map/while/body/eval_jaxpr/transpose | solution.py:59
  668.5 7.1 collective-permute-start.10
  684.0 82.6 %all-reduce.1 = (f32[]{:T(128)}, f32[256,3]{0,1:T(4,128)}) all-reduce(f32[]{:T(128)S(6)} %select_n.311, f32[256,3]{0,1:T(4,128)S(1)} %fusion.48), channel_id=1, replica_groups=mesh['section'=8,'slab'=16] {'section','slab'}, use_global_device_ids=true, to_apply=%region_3.4 | all-reduce | flops 769 | bytes 6152 | tf_op jit(solution)/shard_map/psum | solution.py:167
  767.2 68.0 %all-reduce.5.cloned.1.call-done = (f32[1,3,3,3,256,256]{5,4,3,2,1,0:T(8,128)}, f32[1,256,256]{2,1,0:T(8,128)}) async-done(((f32[1,3,3,3,256,256]{5,4,3,2,1,0:T(8,128)}, f32[1,256,256]{2,1,0:T(8,128)}), (f32[1,3,3,3,256,256]{5,4,3,2,1,0:T(8,128)}, f32[1,256,256]{2,1,0:T(8,128)})) %all-reduce.5.cloned.1.call-update) | async-done | bytes 7340048 | tf_op jit(solution)/shard_map/psum | solution.py:212
  835.2 6.8 copy.128
  (732 shorter events, 465.5 us)
Async XLA Ops:
  7.2 828.0 %all-reduce.5.cloned.1.call-start = ((), (), s32[]{:S(2)}) async-start(), calls=%async_computation | async-start | bytes 14680064 | tf_op jit(solution)/shard_map/psum | solution.py:212
  7.2 29.9 %collective-permute-start.13 = (s32[2,1,2,64]{3,2,0,1:T(2,128)}, s32[2,1,2,64]{3,2,0,1:T(2,128)S(1)}, u32[]{:S(2)}, u32[]{:S(2)}) collective-permute-start(s32[2,1,2,64]{3,2,0,1:T(2,128)} %bitcast.327), channel_id=1, source_target_pairs={{1,0},{2,1},{3,2},{4,3},{5,4},{6,5},{7,6},{8,7},{9,8},{10,9},{11,1... | collective-permute-start | bytes 3080 | tf_op jit(solution)/shard_map/ppermute | solution.py:17
  10.6 26.6 %collective-permute-start.12 = (s32[2,1,2,64]{3,2,0,1:T(2,128)}, s32[2,1,2,64]{3,2,0,1:T(2,128)}, u32[]{:S(2)}, u32[]{:S(2)}) collective-permute-start(s32[2,1,2,64]{3,2,0,1:T(2,128)} %bitcast.328), channel_id=1, source_target_pairs={{0,1},{1,2},{2,3},{3,4},{4,5},{5,6},{6,7},{7,8},{8,9},{9,10},{10,1... | collective-permute-start | bytes 3080 | tf_op jit(solution)/shard_map/ppermute | solution.py:14
  59.6 13.4 %collective-permute-start.2 = (bf16[256,1,2,64]{0,3,2,1:T(8,128)(2,1)S(1)}, bf16[256,1,2,64]{0,3,2,1:T(8,128)(2,1)S(1)}, u32[]{:S(2)}, u32[]{:S(2)}) collective-permute-start(bf16[256,1,2,64]{0,3,2,1:T(8,128)(2,1)S(1)} %fusion.80), channel_id=1, source_target_pairs={{0,16},{16,32},{32,48},{48,64},{64,80},{80,96},{96,112},{1,17},{17... | collective-permute-start | bytes 196616 | tf_op jit(solution)/shard_map/while/body/eval_jaxpr/ppermute | solution.py:25
  92.5 13.8 %collective-permute-start.2 = (bf16[256,1,2,64]{0,3,2,1:T(8,128)(2,1)S(1)}, bf16[256,1,2,64]{0,3,2,1:T(8,128)(2,1)S(1)}, u32[]{:S(2)}, u32[]{:S(2)}) collective-permute-start(bf16[256,1,2,64]{0,3,2,1:T(8,128)(2,1)S(1)} %fusion.80), channel_id=1, source_target_pairs={{0,16},{16,32},{32,48},{48,64},{64,80},{80,96},{96,112},{1,17},{17... | collective-permute-start | bytes 196616 | tf_op jit(solution)/shard_map/while/body/eval_jaxpr/ppermute | solution.py:25
  126.1 12.3 %collective-permute-start.2 = (bf16[256,1,2,64]{0,3,2,1:T(8,128)(2,1)S(1)}, bf16[256,1,2,64]{0,3,2,1:T(8,128)(2,1)S(1)}, u32[]{:S(2)}, u32[]{:S(2)}) collective-permute-start(bf16[256,1,2,64]{0,3,2,1:T(8,128)(2,1)S(1)} %fusion.80), channel_id=1, source_target_pairs={{0,16},{16,32},{32,48},{48,64},{64,80},{80,96},{96,112},{1,17},{17... | collective-permute-start | bytes 196616 | tf_op jit(solution)/shard_map/while/body/eval_jaxpr/ppermute | solution.py:25
  158.0 12.4 %collective-permute-start.2 = (bf16[256,1,2,64]{0,3,2,1:T(8,128)(2,1)S(1)}, bf16[256,1,2,64]{0,3,2,1:T(8,128)(2,1)S(1)}, u32[]{:S(2)}, u32[]{:S(2)}) collective-permute-start(bf16[256,1,2,64]{0,3,2,1:T(8,128)(2,1)S(1)} %fusion.80), channel_id=1, source_target_pairs={{0,16},{16,32},{32,48},{48,64},{64,80},{80,96},{96,112},{1,17},{17... | collective-permute-start | bytes 196616 | tf_op jit(solution)/shard_map/while/body/eval_jaxpr/ppermute | solution.py:25
  189.6 12.2 %collective-permute-start.2 = (bf16[256,1,2,64]{0,3,2,1:T(8,128)(2,1)S(1)}, bf16[256,1,2,64]{0,3,2,1:T(8,128)(2,1)S(1)}, u32[]{:S(2)}, u32[]{:S(2)}) collective-permute-start(bf16[256,1,2,64]{0,3,2,1:T(8,128)(2,1)S(1)} %fusion.80), channel_id=1, source_target_pairs={{0,16},{16,32},{32,48},{48,64},{64,80},{80,96},{96,112},{1,17},{17... | collective-permute-start | bytes 196616 | tf_op jit(solution)/shard_map/while/body/eval_jaxpr/ppermute | solution.py:25
  220.8 12.6 %collective-permute-start.2 = (bf16[256,1,2,64]{0,3,2,1:T(8,128)(2,1)S(1)}, bf16[256,1,2,64]{0,3,2,1:T(8,128)(2,1)S(1)}, u32[]{:S(2)}, u32[]{:S(2)}) collective-permute-start(bf16[256,1,2,64]{0,3,2,1:T(8,128)(2,1)S(1)} %fusion.80), channel_id=1, source_target_pairs={{0,16},{16,32},{32,48},{48,64},{64,80},{80,96},{96,112},{1,17},{17... | collective-permute-start | bytes 196616 | tf_op jit(solution)/shard_map/while/body/eval_jaxpr/ppermute | solution.py:25
  236.6 9.4 %collective-permute-start.1 = (bf16[256,1,2,64]{0,3,2,1:T(8,128)(2,1)}, bf16[256,1,2,64]{0,3,2,1:T(8,128)(2,1)}, u32[]{:S(2)}, u32[]{:S(2)}) collective-permute-start(bf16[256,1,2,64]{0,3,2,1:T(8,128)(2,1)} %get-tuple-element.930), channel_id=1, source_target_pairs={{0,1},{1,2},{2,3},{3,4},{4,5},{5,6},{6,7},{7,8},{8,9},{9,10},{10,1... | collective-permute-start | bytes 196616 | tf_op jit(solution)/shard_map/while/body/eval_jaxpr/ppermute | solution.py:14
  253.8 12.6 %collective-permute-start.2 = (bf16[256,1,2,64]{0,3,2,1:T(8,128)(2,1)S(1)}, bf16[256,1,2,64]{0,3,2,1:T(8,128)(2,1)S(1)}, u32[]{:S(2)}, u32[]{:S(2)}) collective-permute-start(bf16[256,1,2,64]{0,3,2,1:T(8,128)(2,1)S(1)} %fusion.80), channel_id=1, source_target_pairs={{0,16},{16,32},{32,48},{48,64},{64,80},{80,96},{96,112},{1,17},{17... | collective-permute-start | bytes 196616 | tf_op jit(solution)/shard_map/while/body/eval_jaxpr/ppermute | solution.py:25
  269.6 9.3 %collective-permute-start.1 = (bf16[256,1,2,64]{0,3,2,1:T(8,128)(2,1)}, bf16[256,1,2,64]{0,3,2,1:T(8,128)(2,1)}, u32[]{:S(2)}, u32[]{:S(2)}) collective-permute-start(bf16[256,1,2,64]{0,3,2,1:T(8,128)(2,1)} %get-tuple-element.930), channel_id=1, source_target_pairs={{0,1},{1,2},{2,3},{3,4},{4,5},{5,6},{6,7},{7,8},{8,9},{9,10},{10,1... | collective-permute-start | bytes 196616 | tf_op jit(solution)/shard_map/while/body/eval_jaxpr/ppermute | solution.py:14
  286.8 12.6 %collective-permute-start.2 = (bf16[256,1,2,64]{0,3,2,1:T(8,128)(2,1)S(1)}, bf16[256,1,2,64]{0,3,2,1:T(8,128)(2,1)S(1)}, u32[]{:S(2)}, u32[]{:S(2)}) collective-permute-start(bf16[256,1,2,64]{0,3,2,1:T(8,128)(2,1)S(1)} %fusion.80), channel_id=1, source_target_pairs={{0,16},{16,32},{32,48},{48,64},{64,80},{80,96},{96,112},{1,17},{17... | collective-permute-start | bytes 196616 | tf_op jit(solution)/shard_map/while/body/eval_jaxpr/ppermute | solution.py:25
  302.6 10.5 %collective-permute-start.1 = (bf16[256,1,2,64]{0,3,2,1:T(8,128)(2,1)}, bf16[256,1,2,64]{0,3,2,1:T(8,128)(2,1)}, u32[]{:S(2)}, u32[]{:S(2)}) collective-permute-start(bf16[256,1,2,64]{0,3,2,1:T(8,128)(2,1)} %get-tuple-element.930), channel_id=1, source_target_pairs={{0,1},{1,2},{2,3},{3,4},{4,5},{5,6},{6,7},{7,8},{8,9},{9,10},{10,1... | collective-permute-start | bytes 196616 | tf_op jit(solution)/shard_map/while/body/eval_jaxpr/ppermute | solution.py:14
  320.2 13.4 %collective-permute-start.2 = (bf16[256,1,2,64]{0,3,2,1:T(8,128)(2,1)S(1)}, bf16[256,1,2,64]{0,3,2,1:T(8,128)(2,1)S(1)}, u32[]{:S(2)}, u32[]{:S(2)}) collective-permute-start(bf16[256,1,2,64]{0,3,2,1:T(8,128)(2,1)S(1)} %fusion.80), channel_id=1, source_target_pairs={{0,16},{16,32},{32,48},{48,64},{64,80},{80,96},{96,112},{1,17},{17... | collective-permute-start | bytes 196616 | tf_op jit(solution)/shard_map/while/body/eval_jaxpr/ppermute | solution.py:25
  338.0 9.4 %collective-permute-start.7 = (bf16[256,1,2,64]{0,3,2,1:T(8,128)(2,1)S(1)}, bf16[256,1,2,64]{0,3,2,1:T(8,128)(2,1)S(1)}, u32[]{:S(2)}, u32[]{:S(2)}) collective-permute-start(bf16[256,1,2,64]{0,3,2,1:T(8,128)(2,1)S(1)} %fusion.90), channel_id=1, source_target_pairs={{0,1},{1,2},{2,3},{3,4},{4,5},{5,6},{6,7},{7,8},{8,9},{9,10},{10,1... | collective-permute-start | bytes 196616 | tf_op jit(solution)/shard_map/while/body/eval_jaxpr/ppermute | solution.py:14
  385.4 10.7 %collective-permute-start.9 = (bf16[256,1,2,64]{0,3,2,1:T(8,128)(2,1)S(1)}, bf16[256,1,2,64]{0,3,2,1:T(8,128)(2,1)S(1)}, u32[]{:S(2)}, u32[]{:S(2)}) collective-permute-start(bf16[256,1,2,64]{0,3,2,1:T(8,128)(2,1)S(1)} %get-tuple-element.951), channel_id=1, source_target_pairs={{0,16},{16,0},{32,48},{48,32},{64,80},{80,64},{96,112},{112,96},{1... | collective-permute-start | bytes 196616 | tf_op jit(solution)/shard_map/while/body/eval_jaxpr/ppermute | solution.py:35
  424.6 8.8 %collective-permute-start.9 = (bf16[256,1,2,64]{0,3,2,1:T(8,128)(2,1)S(1)}, bf16[256,1,2,64]{0,3,2,1:T(8,128)(2,1)S(1)}, u32[]{:S(2)}, u32[]{:S(2)}) collective-permute-start(bf16[256,1,2,64]{0,3,2,1:T(8,128)(2,1)S(1)} %get-tuple-element.951), channel_id=1, source_target_pairs={{0,16},{16,0},{32,48},{48,32},{64,80},{80,64},{96,112},{112,96},{1... | collective-permute-start | bytes 196616 | tf_op jit(solution)/shard_map/while/body/eval_jaxpr/ppermute | solution.py:35
  447.9 9.1 %collective-permute-start.7 = (bf16[256,1,2,64]{0,3,2,1:T(8,128)(2,1)S(1)}, bf16[256,1,2,64]{0,3,2,1:T(8,128)(2,1)S(1)}, u32[]{:S(2)}, u32[]{:S(2)}) collective-permute-start(bf16[256,1,2,64]{0,3,2,1:T(8,128)(2,1)S(1)} %fusion.90), channel_id=1, source_target_pairs={{0,1},{1,2},{2,3},{3,4},{4,5},{5,6},{6,7},{7,8},{8,9},{9,10},{10,1... | collective-permute-start | bytes 196616 | tf_op jit(solution)/shard_map/while/body/eval_jaxpr/ppermute | solution.py:14
  463.2 8.8 %collective-permute-start.9 = (bf16[256,1,2,64]{0,3,2,1:T(8,128)(2,1)S(1)}, bf16[256,1,2,64]{0,3,2,1:T(8,128)(2,1)S(1)}, u32[]{:S(2)}, u32[]{:S(2)}) collective-permute-start(bf16[256,1,2,64]{0,3,2,1:T(8,128)(2,1)S(1)} %get-tuple-element.951), channel_id=1, source_target_pairs={{0,16},{16,0},{32,48},{48,32},{64,80},{80,64},{96,112},{112,96},{1... | collective-permute-start | bytes 196616 | tf_op jit(solution)/shard_map/while/body/eval_jaxpr/ppermute | solution.py:35
  472.0 8.8 %collective-permute-start.10 = (bf16[256,1,2,64]{0,3,2,1:T(8,128)(2,1)S(1)}, bf16[256,1,2,64]{0,3,2,1:T(8,128)(2,1)S(1)}, u32[]{:S(2)}, u32[]{:S(2)}) collective-permute-start(bf16[256,1,2,64]{0,3,2,1:T(8,128)(2,1)S(1)} %collective-permute-done.9), channel_id=1, source_target_pairs={{0,32},{32,0},{16,48},{48,16},{64,96},{96,64},{80,112},{112,80},{1... | collective-permute-start | bytes 196616 | tf_op jit(solution)/shard_map/while/body/eval_jaxpr/ppermute | solution.py:35
  486.8 9.4 %collective-permute-start.7 = (bf16[256,1,2,64]{0,3,2,1:T(8,128)(2,1)S(1)}, bf16[256,1,2,64]{0,3,2,1:T(8,128)(2,1)S(1)}, u32[]{:S(2)}, u32[]{:S(2)}) collective-permute-start(bf16[256,1,2,64]{0,3,2,1:T(8,128)(2,1)S(1)} %fusion.90), channel_id=1, source_target_pairs={{0,1},{1,2},{2,3},{3,4},{4,5},{5,6},{6,7},{7,8},{8,9},{9,10},{10,1... | collective-permute-start | bytes 196616 | tf_op jit(solution)/shard_map/while/body/eval_jaxpr/ppermute | solution.py:14
  502.4 8.8 %collective-permute-start.9 = (bf16[256,1,2,64]{0,3,2,1:T(8,128)(2,1)S(1)}, bf16[256,1,2,64]{0,3,2,1:T(8,128)(2,1)S(1)}, u32[]{:S(2)}, u32[]{:S(2)}) collective-permute-start(bf16[256,1,2,64]{0,3,2,1:T(8,128)(2,1)S(1)} %get-tuple-element.951), channel_id=1, source_target_pairs={{0,16},{16,0},{32,48},{48,32},{64,80},{80,64},{96,112},{112,96},{1... | collective-permute-start | bytes 196616 | tf_op jit(solution)/shard_map/while/body/eval_jaxpr/ppermute | solution.py:35
  526.0 9.8 %collective-permute-start.7 = (bf16[256,1,2,64]{0,3,2,1:T(8,128)(2,1)S(1)}, bf16[256,1,2,64]{0,3,2,1:T(8,128)(2,1)S(1)}, u32[]{:S(2)}, u32[]{:S(2)}) collective-permute-start(bf16[256,1,2,64]{0,3,2,1:T(8,128)(2,1)S(1)} %fusion.90), channel_id=1, source_target_pairs={{0,1},{1,2},{2,3},{3,4},{4,5},{5,6},{6,7},{7,8},{8,9},{9,10},{10,1... | collective-permute-start | bytes 196616 | tf_op jit(solution)/shard_map/while/body/eval_jaxpr/ppermute | solution.py:14
  541.9 8.8 %collective-permute-start.9 = (bf16[256,1,2,64]{0,3,2,1:T(8,128)(2,1)S(1)}, bf16[256,1,2,64]{0,3,2,1:T(8,128)(2,1)S(1)}, u32[]{:S(2)}, u32[]{:S(2)}) collective-permute-start(bf16[256,1,2,64]{0,3,2,1:T(8,128)(2,1)S(1)} %get-tuple-element.951), channel_id=1, source_target_pairs={{0,16},{16,0},{32,48},{48,32},{64,80},{80,64},{96,112},{112,96},{1... | collective-permute-start | bytes 196616 | tf_op jit(solution)/shard_map/while/body/eval_jaxpr/ppermute | solution.py:35
  565.5 9.4 %collective-permute-start.7 = (bf16[256,1,2,64]{0,3,2,1:T(8,128)(2,1)S(1)}, bf16[256,1,2,64]{0,3,2,1:T(8,128)(2,1)S(1)}, u32[]{:S(2)}, u32[]{:S(2)}) collective-permute-start(bf16[256,1,2,64]{0,3,2,1:T(8,128)(2,1)S(1)} %fusion.90), channel_id=1, source_target_pairs={{0,1},{1,2},{2,3},{3,4},{4,5},{5,6},{6,7},{7,8},{8,9},{9,10},{10,1... | collective-permute-start | bytes 196616 | tf_op jit(solution)/shard_map/while/body/eval_jaxpr/ppermute | solution.py:14
  581.1 8.8 %collective-permute-start.9 = (bf16[256,1,2,64]{0,3,2,1:T(8,128)(2,1)S(1)}, bf16[256,1,2,64]{0,3,2,1:T(8,128)(2,1)S(1)}, u32[]{:S(2)}, u32[]{:S(2)}) collective-permute-start(bf16[256,1,2,64]{0,3,2,1:T(8,128)(2,1)S(1)} %get-tuple-element.951), channel_id=1, source_target_pairs={{0,16},{16,0},{32,48},{48,32},{64,80},{80,64},{96,112},{112,96},{1... | collective-permute-start | bytes 196616 | tf_op jit(solution)/shard_map/while/body/eval_jaxpr/ppermute | solution.py:35
  604.6 9.8 %collective-permute-start.7 = (bf16[256,1,2,64]{0,3,2,1:T(8,128)(2,1)S(1)}, bf16[256,1,2,64]{0,3,2,1:T(8,128)(2,1)S(1)}, u32[]{:S(2)}, u32[]{:S(2)}) collective-permute-start(bf16[256,1,2,64]{0,3,2,1:T(8,128)(2,1)S(1)} %fusion.90), channel_id=1, source_target_pairs={{0,1},{1,2},{2,3},{3,4},{4,5},{5,6},{6,7},{7,8},{8,9},{9,10},{10,1... | collective-permute-start | bytes 196616 | tf_op jit(solution)/shard_map/while/body/eval_jaxpr/ppermute | solution.py:14
  620.6 8.8 %collective-permute-start.9 = (bf16[256,1,2,64]{0,3,2,1:T(8,128)(2,1)S(1)}, bf16[256,1,2,64]{0,3,2,1:T(8,128)(2,1)S(1)}, u32[]{:S(2)}, u32[]{:S(2)}) collective-permute-start(bf16[256,1,2,64]{0,3,2,1:T(8,128)(2,1)S(1)} %get-tuple-element.951), channel_id=1, source_target_pairs={{0,16},{16,0},{32,48},{48,32},{64,80},{80,64},{96,112},{112,96},{1... | collective-permute-start | bytes 196616 | tf_op jit(solution)/shard_map/while/body/eval_jaxpr/ppermute | solution.py:35
  644.2 9.4 %collective-permute-start.7 = (bf16[256,1,2,64]{0,3,2,1:T(8,128)(2,1)S(1)}, bf16[256,1,2,64]{0,3,2,1:T(8,128)(2,1)S(1)}, u32[]{:S(2)}, u32[]{:S(2)}) collective-permute-start(bf16[256,1,2,64]{0,3,2,1:T(8,128)(2,1)S(1)} %fusion.90), channel_id=1, source_target_pairs={{0,1},{1,2},{2,3},{3,4},{4,5},{5,6},{6,7},{7,8},{8,9},{9,10},{10,1... | collective-permute-start | bytes 196616 | tf_op jit(solution)/shard_map/while/body/eval_jaxpr/ppermute | solution.py:14
  659.7 8.8 %collective-permute-start.9 = (bf16[256,1,2,64]{0,3,2,1:T(8,128)(2,1)S(1)}, bf16[256,1,2,64]{0,3,2,1:T(8,128)(2,1)S(1)}, u32[]{:S(2)}, u32[]{:S(2)}) collective-permute-start(bf16[256,1,2,64]{0,3,2,1:T(8,128)(2,1)S(1)} %get-tuple-element.951), channel_id=1, source_target_pairs={{0,16},{16,0},{32,48},{48,32},{64,80},{80,64},{96,112},{112,96},{1... | collective-permute-start | bytes 196616 | tf_op jit(solution)/shard_map/while/body/eval_jaxpr/ppermute | solution.py:35
  668.5 8.8 %collective-permute-start.10 = (bf16[256,1,2,64]{0,3,2,1:T(8,128)(2,1)S(1)}, bf16[256,1,2,64]{0,3,2,1:T(8,128)(2,1)S(1)}, u32[]{:S(2)}, u32[]{:S(2)}) collective-permute-start(bf16[256,1,2,64]{0,3,2,1:T(8,128)(2,1)S(1)} %collective-permute-done.9), channel_id=1, source_target_pairs={{0,32},{32,0},{16,48},{48,16},{64,96},{96,64},{80,112},{112,80},{1... | collective-permute-start | bytes 196616 | tf_op jit(solution)/shard_map/while/body/eval_jaxpr/ppermute | solution.py:35
  (194 other events, 2042.4 us)
Sparse Core Ops, SparseCore 0:
  682.4 152.7 all-reduce.4
where the time goes:
time: 856 us; the launch traced here: 851 us
  starting transfers between devices  281 us (33%)
  waiting for transfers between devices  218 us (25%)
  matrix products  129 us (15%)
  blocking collectives  82.6 us (10%)
  local copies, waits for them, and re-layouts  64.7 us (8%)
  other arithmetic  44.1 us (5%)
  between operations  27.9 us (3%)
    ppermute x19, starting transfers between devices, extended(): lax.ppermute(lax.slice_in_dim(block, block.shape[dim] - width, None, axis...  106 us
    ppermute x54, starting transfers between devices, partner(): return lax.ppermute(block, axis, route)  105 us
    ppermute x54, waiting for transfers between devices, partner(): return lax.ppermute(block, axis, route)  94.2 us
    psum x1, blocking collectives, body(): loss_sum, grad_head = lax.psum((loss_part, head_part), ('section', 'slab'))  82.6 us
    transpose x9, matrix products, weight_grad(): return jnp.transpose(result, (2, 3, 4, 0, 1))  75 us
    psum x1, waiting for transfers between devices, body(): grad_kernel, grad_mixing = lax.psum((loop_state[2], loop_state[3]), 'slab')  68 us
    ppermute x19, waiting for transfers between devices, extended(): lax.ppermute(lax.slice_in_dim(block, 0, width, axis=dim), axis, backward)  49.8 us
    ppermute x19, starting transfers between devices, extended(): lax.ppermute(lax.slice_in_dim(block, 0, width, axis=dim), axis, backward)  38.5 us
  transfers between devices with their start and end apart: 111, of which 64 were waited for; matrix products, arithmetic and copies ran while one was open for 14% of the time, Pallas kernels for 0%

commit v1 on v0

v1 whole, which is shorter than its diff:
```python
import functools

import jax
import jax.numpy as jnp
from jax import lax
from jax.experimental import pallas as pl
from jax.experimental.pallas import tpu as pltpu
from jax.sharding import PartitionSpec as P

loss_scale = 1024.0
MESH = pl.DeviceIdType.MESH
F32 = jnp.float32
BF16 = jnp.bfloat16


STAGE, HEADS, SUMS = 0, 1, 2
PEERS, TWIN = 3, 6
BASE, STRIDE = 9, 8
MAIN, LEFT, RIGHT, MIRROR, DOWN, SKIP, GLEFT, GRIGHT = range(8)


def dot(a, b):
    return jnp.dot(a, b, preferred_element_type=F32)


def dot_nt(a, b):
    return lax.dot_general(a, b, (((1,), (1,)), ((), ())), preferred_element_type=F32)


def shifted(value, by):
    rows = value.shape[0]
    depth = lax.broadcasted_iota(jnp.int32, value.shape, 0) & 15
    rolled = pltpu.roll(value, (rows - by) % rows, 0)
    inside = depth < 15 if by > 0 else depth > 0
    return jnp.where(inside, rolled, 0.0)


def chain_kernel(
    count,
    pay,
    weight,
    mixing,
    head,
    head_t,
    offs,
    xg,
    bg,
    pg,
    sums,
    stage,
    xc,
    bc,
    ys,
    pre,
    cot,
    labs,
    down_in,
    down_out,
    skip_in,
    skip_out,
    pgc,
    heads,
    total,
    ssem,
    rsem,
):
    sec = lax.axis_index("section")
    me = lax.axis_index("slab")
    chip = me // 2
    core = me % 2
    micro = 2

    def remote(src, dst, index, device):
        return pltpu.make_async_remote_copy(
            src_ref=src,
            dst_ref=dst,
            send_sem=ssem.at[index],
            recv_sem=rsem.at[index],
            device_id=device,
            device_id_type=MESH,
        )

    has_left = me > 0
    has_right = me < 15
    to_left = jnp.maximum(me - 1, 0)
    to_right = jnp.minimum(me + 1, 15)

    def stage_copy(peer):
        return remote(pay.at[peer], stage.at[me], STAGE, (sec, peer))

    @pl.when((sec == 0) | (sec == 7))
    def _():
        def send(step, carry):
            stage_copy((me + step) % 16).start()
            return carry

        lax.fori_loop(1, 16, send, 0)
        stage[me] = pay[me]

    @pl.when(me == 0)
    def _():
        xc[:, :, 0:16, :] = jnp.zeros((2, 2, 16, 256), BF16)
        pgc[:, :, 0:16, :] = jnp.zeros((2, 2, 16, 256), BF16)

    @pl.when(me == 15)
    def _():
        xc[:, :, 80:96, :] = jnp.zeros((2, 2, 16, 256), BF16)
        pgc[:, :, 80:96, :] = jnp.zeros((2, 2, 16, 256), BF16)

    @pl.when((sec == 0) | (sec == 7))
    def _():
        all_staged = remote(stage.at[pl.ds(0, 15)], stage.at[pl.ds(0, 15)], STAGE, (sec, to_left))
        all_staged.wait_send()
        all_staged.wait_recv()
        out_row = lax.broadcasted_iota(jnp.int32, (192, 256), 0)
        in_row = lax.broadcasted_iota(jnp.int32, (192, 256), 1)
        second = (out_row >= 96).astype(jnp.int32)
        rest = out_row - 96 * second
        column = rest >> 4
        depth = rest & 15
        perm = jnp.where(in_row == depth * 16 + second * 8 + column + 1, 1.0, 0.0).astype(BF16)
        for m in range(2):
            block = dot(perm, stage[:, m].reshape(256, 256))

            @pl.when(sec == 0)
            def _():
                xc[m] = block.astype(BF16).reshape(2, 96, 256)

            @pl.when(sec == 7)
            def _():
                labs[m] = block[:, :128]

    def forward_copies(m):
        base = BASE + STRIDE * m
        up = jnp.minimum(sec + 1, 7)
        main = remote(ys.at[m], xc.at[m, :, pl.ds(16, 64)], base + MAIN, (up, me))
        left = remote(
            ys.at[m, :, pl.ds(0, 16)], xc.at[m, :, pl.ds(80, 16)], base + LEFT, (up, to_left)
        )
        right = remote(
            ys.at[m, :, pl.ds(48, 16)], xc.at[m, :, pl.ds(0, 16)], base + RIGHT, (up, to_right)
        )
        mirror = remote(ys.at[m], bc.at[m], base + MIRROR, (7 - sec, me))
        return main, left, right, mirror

    def forward(m, carry):
        main, left, right, mirror = forward_copies(m)

        @pl.when(sec > 0)
        def _():
            main.wait_recv()

            @pl.when(has_right)
            def _():
                left.wait_recv()

            @pl.when(has_left)
            def _():
                right.wait_recv()

        @pl.when(sec <= 4)
        def _():
            bc[m] = xc[m, :, 16:80, :]

        parts = []
        for kd in range(3):
            same = top = bottom = None
            for kc in range(3):
                both = xc[m, :, 16 * kc : 16 * kc + 64, :]
                part = dot(both.reshape(128, 256), weight[kd, 1, kc])
                high = dot(both[1], weight[kd, 2, kc])
                low = dot(both[0], weight[kd, 0, kc])
                same = part if same is None else same + part
                top = high if top is None else top + high
                bottom = low if bottom is None else bottom + low
            parts.append(same + jnp.concatenate([top, bottom], axis=0))

        @pl.when(sec >= 5)
        def _():
            mirror.wait_recv()

        preact = parts[1] + shifted(parts[0], -1) + shifted(parts[2], 1)
        preact = preact + dot(bc[m].reshape(128, 256), mixing[...])
        pre[m] = preact
        output = (preact / (1.0 + jnp.exp(-preact))).astype(BF16)
        ys[m] = output.reshape(2, 64, 256)

        @pl.when(sec < 7)
        def _():
            @pl.when(has_left)
            def _():
                left.start()

            @pl.when(has_right)
            def _():
                right.start()

            main.start()

        @pl.when(sec < 3)
        def _():
            mirror.start()

        @pl.when(sec == 7)
        def _():
            logits = dot(output, head[...])
            label = labs[m]
            along_depth, along_row, along_col = offs[0:1, :], offs[1:2, :], offs[2:3, :]
            near = jnp.where(
                along_depth < 0.0,
                shifted(label, -1),
                jnp.where(along_depth > 0.0, shifted(label, 1), label),
            )
            rows = []
            for r in range(2):
                start = 96 * r
                rows.append(
                    jnp.where(
                        along_col < 0.0,
                        near[start : start + 64],
                        jnp.where(
                            along_col > 0.0,
                            near[start + 32 : start + 96],
                            near[start + 16 : start + 80],
                        ),
                    )
                )
            zero = jnp.zeros((64, 128), F32)
            first = jnp.where(
                along_row < 0.0, zero, jnp.where(along_row > 0.0, rows[1], rows[0])
            )
            second = jnp.where(
                along_row > 0.0, zero, jnp.where(along_row < 0.0, rows[0], rows[1])
            )
            neighbor = jnp.concatenate([first, second], axis=0)
            own = jnp.concatenate([label[16:80], label[112:176]], axis=0)
            target = jnp.where((neighbor == own) & (own != 0.0), 1.0, 0.0)
            lane = lax.broadcasted_iota(jnp.int32, (128, 128), 1)
            channel = lane < 3
            soft = jnp.maximum(logits, 0.0) + jnp.log1p(jnp.exp(-jnp.abs(logits)))
            loss = jnp.sum(jnp.where(channel, soft - target * logits, 0.0))
            sigma = 1.0 / (1.0 + jnp.exp(-logits))
            grad = jnp.where(channel, loss_scale * (sigma - target) / count, 0.0)
            rounded = grad.astype(BF16)
            cot[m] = dot(rounded, head_t[...])
            across = rounded.astype(F32).T.astype(BF16)
            grad_head = dot(across, output)[0:8]
            row = lax.broadcasted_iota(jnp.int32, (8, 256), 0)
            partial = jnp.where(row == 3, loss, grad_head)

            @pl.when(m == 0)
            def _():
                heads[me] = partial

            @pl.when(m > 0)
            def _():
                heads[me] = heads[me] + partial

        return carry

    lax.fori_loop(0, micro, forward, 0)

    def gather(out, which):
        def to_peer(peer):
            block = out.at[core, chip]
            return remote(block, block, PEERS + which, (sec, peer * 2 + core))

        def send(step, carry):
            to_peer((chip + step) % 8).start()
            return carry

        lax.fori_loop(1, 8, send, 0)

    def gather_twin(out, which):
        seven = out.at[core, pl.ds(0, 7)]
        peers = remote(seven, seven, PEERS + which, (sec, (chip + 1) % 8 * 2 + core))
        peers.wait_send()
        peers.wait_recv()
        twin = remote(out.at[core], out.at[core], TWIN + which, (sec, chip * 2 + 1 - core))
        twin.start()

    def gather_end(out, which):
        twin = remote(out.at[core], out.at[core], TWIN + which, (sec, chip * 2 + 1 - core))
        twin.wait_send()
        twin.wait_recv()

    def gather_inputs():
        for m in range(2):
            xg[core, chip, m] = xc[m, :, 16:80, :]
        gather(xg, 0)

        @pl.when(sec >= 5)
        def _():
            for m in range(2):
                bg[core, chip, m] = bc[m]
            gather(bg, 1)

        gather_twin(xg, 0)

        @pl.when(sec >= 5)
        def _():
            gather_twin(bg, 1)
            gather_end(bg, 1)

        gather_end(xg, 0)

    @pl.when(sec < 4)
    def _():
        gather_inputs()

    def backward_copies(m):
        base = BASE + STRIDE * m
        down = remote(down_out.at[m], down_in.at[m], base + DOWN, (jnp.maximum(sec - 1, 0), me))
        skip = remote(skip_out.at[m], skip_in.at[m], base + SKIP, (7 - sec, me))
        left = remote(
            pgc.at[m, :, pl.ds(16, 16)], pgc.at[m, :, pl.ds(80, 16)], base + GLEFT, (sec, to_left)
        )
        right = remote(
            pgc.at[m, :, pl.ds(64, 16)], pgc.at[m, :, pl.ds(0, 16)], base + GRIGHT, (sec, to_right)
        )
        return down, skip, left, right

    def backward(m, carry):
        down, skip, left, right = backward_copies(m)

        @pl.when(sec < 7)
        def _():
            down.wait_recv()
            cot[m] = down_in[m].reshape(128, 256).astype(F32)

        @pl.when(sec < 4)
        def _():
            skip.wait_recv()
            cot[m] = cot[m] + skip_in[m].reshape(128, 256).astype(F32)

        preact = pre[m]
        sigma = 1.0 / (1.0 + jnp.exp(-preact))
        grad = (cot[m] * (sigma * (1.0 + preact * (1.0 - sigma)))).astype(BF16)
        pgc[m, :, 16:80, :] = grad.reshape(2, 64, 256)

        @pl.when(sec > 0)
        def _():
            @pl.when(has_left)
            def _():
                left.start()

            @pl.when(has_right)
            def _():
                right.start()

            branch = dot_nt(grad, mixing[...])

            @pl.when(sec >= 4)
            def _():
                skip_out[m] = branch.astype(BF16).reshape(2, 64, 256)
                skip.start()

            def column(kc, sums_of):
                both = pgc[m, :, 16 * (2 - kc) : 16 * (2 - kc) + 64, :]
                flat = both.reshape(128, 256)
                result = []
                for kd in range(3):
                    same = dot_nt(flat, weight[kd, 1, kc])
                    high = dot_nt(both[1], weight[kd, 0, kc])
                    low = dot_nt(both[0], weight[kd, 2, kc])
                    part = same + jnp.concatenate([high, low], axis=0)
                    result.append(part if sums_of is None else sums_of[kd] + part)
                return result

            parts = column(1, None)

            @pl.when(has_right)
            def _():
                left.wait_recv()

            @pl.when(has_left)
            def _():
                right.wait_recv()

            parts = column(2, column(0, parts))
            result = parts[1] + shifted(parts[0], 1) + shifted(parts[2], -1)
            result = jnp.where(sec < 4, result + branch, result)
            down_out[m] = result.astype(BF16).reshape(2, 64, 256)
            down.start()

        return carry

    lax.fori_loop(0, micro, backward, 0)

    for m in range(2):
        pg[core, chip, m] = pgc[m, :, 16:80, :]
    gather(pg, 2)

    def head_copy(peer):
        return remote(heads.at[me], heads.at[me], HEADS, (7, peer))

    def sum_copy(other):
        return remote(total, sums, SUMS, (other, me))

    @pl.when(sec == 7)
    def _():
        def send(step, carry):
            head_copy((me + step) % 16).start()
            return carry

        lax.fori_loop(1, 16, send, 0)
        all_heads = remote(heads.at[pl.ds(0, 15)], heads.at[pl.ds(0, 15)], HEADS, (7, to_left))
        all_heads.wait_send()
        all_heads.wait_recv()
        whole = heads[0]
        for k in range(1, 16):
            whole = whole + heads[k]
        total[...] = whole
        sums[...] = whole

        def spread(other, carry):
            sum_copy(other).start()
            return carry

        lax.fori_loop(0, 7, spread, 0)

    gather_twin(pg, 2)

    @pl.when(sec >= 4)
    def _():
        gather_inputs()

    gather_end(pg, 2)

    @pl.when(sec == 7)
    def _():
        def ended(other, carry):
            sum_copy(other).wait_send()
            return carry

        lax.fori_loop(0, 7, ended, 0)

    @pl.when(sec < 7)
    def _():
        sum_copy(7).wait_recv()

    def finish(m, carry):
        main, left, right, mirror = forward_copies(m)
        down, skip, grad_left, grad_right = backward_copies(m)

        @pl.when(sec < 7)
        def _():
            main.wait_send()

            @pl.when(has_left)
            def _():
                left.wait_send()

            @pl.when(has_right)
            def _():
                right.wait_send()

        @pl.when(sec < 3)
        def _():
            mirror.wait_send()

        @pl.when(sec > 0)
        def _():
            down.wait_send()

            @pl.when(has_left)
            def _():
                grad_left.wait_send()

            @pl.when(has_right)
            def _():
                grad_right.wait_send()

        @pl.when(sec >= 4)
        def _():
            skip.wait_send()

        return carry

    lax.fori_loop(0, micro, finish, 0)


def grads_kernel(xg, bg, pg, out, out_mix, xt, bt, pgs):
    sec = lax.axis_index("section")
    kd = pl.program_id(0)
    kc = pl.program_id(1)

    @pl.when((kd == 0) & (kc == 0))
    def _():
        def turn(step, carry):
            for m in range(2):
                for r in range(2):
                    lanes = pl.ds(pl.multiple_of(step * 128, 128), 128)
                    block = jnp.concatenate([xg[0, step, m, r], xg[1, step, m, r]], axis=0)
                    flipped = block.astype(F32).T.astype(BF16)
                    xt[m, 256 * r : 256 * r + 256, lanes] = flipped

                    @pl.when(sec >= 5)
                    def _():
                        other = jnp.concatenate([bg[0, step, m, r], bg[1, step, m, r]], axis=0)
                        bt[m, r, :, lanes] = other.astype(F32).T.astype(BF16)

                    @pl.when(sec < 5)
                    def _():
                        bt[m, r, :, lanes] = flipped

                    both = jnp.concatenate([pg[0, step, m, r], pg[1, step, m, r]], axis=0)
                    wide = both.astype(F32)
                    rows = pl.ds(pl.multiple_of(16 + step * 128, 16), 128)
                    pgs[0, m, r, rows, :] = shifted(wide, 1).astype(BF16)
                    pgs[1, m, r, rows, :] = both
                    pgs[2, m, r, rows, :] = shifted(wide, -1).astype(BF16)
            return carry

        lax.fori_loop(0, 8, turn, 0)
        for k in range(3):
            for m in range(2):
                for r in range(2):
                    pgs[k, m, r, 0:16, :] = jnp.zeros((16, 256), BF16)
                    pgs[k, m, r, 1040:1056, :] = jnp.zeros((16, 256), BF16)
        mix = None
        for m in range(2):
            for r in range(2):
                part = dot(bt[m, r], pgs[1, m, r, 16:1040, :])
                mix = part if mix is None else mix + part
        out_mix[...] = mix

    rows = pl.ds(pl.multiple_of((2 - kc) * 16, 16), 1024)
    first = dot(xt[0], pgs[kd, 0, 0, rows, :]) + dot(xt[1], pgs[kd, 1, 0, rows, :])
    second = dot(xt[0], pgs[kd, 0, 1, rows, :]) + dot(xt[1], pgs[kd, 1, 1, rows, :])
    out[0, 0, 0] = second[:256]
    out[0, 1, 0] = first[:256] + second[256:]
    out[0, 2, 0] = first[256:]


def payload(features_in, labels):
    slabs = lax.axis_size("slab")

    def windows(value):
        padded = jnp.pad(value, ((0, 0), (0, 0), (2, 2), (0, 0)))
        fours = padded.reshape(2, 2, slabs + 1, 4, value.shape[3])
        eights = jnp.concatenate([fours[:, :, :-1], fours[:, :, 1:]], axis=3)
        return jnp.transpose(eights, (2, 0, 1, 3, 4)).reshape(slabs, 2, 16, value.shape[3])

    features = windows(jnp.transpose(features_in[:, :, 0], (0, 2, 3, 1)))
    ids = windows(labels[:, 0, :, :, None].astype(BF16))
    return jnp.where(lax.axis_index("section") == 7, ids, features)


def body(features_in, labels, offsets, conv_weight, branch_weight, head_weight):
    micro, channels = features_in.shape[0], features_in.shape[1]
    outs = offsets.shape[0]
    cells = features_in.shape[2] * features_in.shape[3] * features_in.shape[4]
    count = micro * outs * cells * lax.axis_size("slab")
    head = jnp.pad(head_weight, ((0, 0), (0, 128 - outs)))
    offs = jnp.pad(offsets.T.astype(F32), ((0, 8 - outs), (0, 128 - outs)))
    vmem = pl.BlockSpec(memory_space=pltpu.VMEM)
    gathered = jax.ShapeDtypeStruct((2, 8, micro, 2, 64, channels), BF16)
    block = (micro, 2, 64, channels)
    xg, bg, pg, sums = pl.pallas_call(
        functools.partial(chain_kernel, float(count)),
        out_shape=(gathered, gathered, gathered, jax.ShapeDtypeStruct((8, channels), F32)),
        in_specs=[vmem] * 6,
        out_specs=(vmem,) * 4,
        scratch_shapes=[
            pltpu.VMEM((16, micro, 16, channels), BF16),
            pltpu.VMEM((micro, 2, 96, channels), BF16),
            pltpu.VMEM(block, BF16),
            pltpu.VMEM(block, BF16),
            pltpu.VMEM((micro, 128, channels), F32),
            pltpu.VMEM((micro, 128, channels), F32),
            pltpu.VMEM((micro, 192, 128), F32),
            pltpu.VMEM(block, BF16),
            pltpu.VMEM(block, BF16),
            pltpu.VMEM(block, BF16),
            pltpu.VMEM(block, BF16),
            pltpu.VMEM((micro, 2, 96, channels), BF16),
            pltpu.VMEM((16, 8, channels), F32),
            pltpu.VMEM((8, channels), F32),
            pltpu.SemaphoreType.DMA((BASE + STRIDE * 2,)),
            pltpu.SemaphoreType.DMA((BASE + STRIDE * 2,)),
        ],
        compiler_params=pltpu.CompilerParams(
            has_side_effects=True, vmem_limit_bytes=40 * 1024 * 1024
        ),
        name="chain",
    )(payload(features_in, labels), conv_weight[0], branch_weight[0], head, head.T, offs)

    grad_kernel, grad_mixing = pl.pallas_call(
        grads_kernel,
        grid=(3, 3),
        out_shape=(
            jax.ShapeDtypeStruct((3, 3, 3, channels, channels), F32),
            jax.ShapeDtypeStruct((channels, channels), F32),
        ),
        in_specs=[vmem] * 3,
        out_specs=(
            pl.BlockSpec((1, 3, 1, channels, channels), lambda kd, kc: (kd, 0, kc, 0, 0)),
            pl.BlockSpec((channels, channels), lambda kd, kc: (0, 0)),
        ),
        scratch_shapes=[
            pltpu.VMEM((micro, 512, 1024), BF16),
            pltpu.VMEM((micro, 2, 256, 1024), BF16),
            pltpu.VMEM((3, micro, 2, 1056, channels), BF16),
        ],
        compiler_params=pltpu.CompilerParams(vmem_limit_bytes=40 * 1024 * 1024),
        name="grads",
    )(xg, bg, pg)
    return (sums[3, 0] / count, grad_kernel[None], grad_mixing[None], sums[:outs].T)


def solution(mesh):
    placed = (
        P(None, None, "slab", None, None),
        P(None, "slab", None, None),
        P(),
        P("section", None, None, None, None, None),
        P("section", None, None),
        P(),
    )
    return jax.shard_map(
        body,
        mesh=mesh,
        in_specs=placed,
        out_specs=(P(), P("section", None, None, None, None, None), P("section", None, None), P()),
        check_vma=False,
    )
```

time: 856 us -> 164 us (0.19)
  starting transfers between devices: 281 us -> 0 us
  waiting for transfers between devices: 218 us -> 0 us
  Pallas kernels: 0 us -> 152 us
  matrix products: 129 us -> 0 us
  blocking collectives: 82.6 us -> 0 us
  local copies, waits for them, and re-layouts: 64.7 us -> 7.06 us
  other arithmetic: 44.1 us -> 1.29 us
  between operations: 27.9 us -> 2.51 us
    ppermute x110 -> x0, starting transfers between devices: 281 us -> none  [the longest x19 106 us: extended(): lax.ppermute(lax.slice_in_dim(block, block.shape[dim] - width, None, axis...]
    pallas_call x0 -> x2, Pallas kernels: none -> 152 us  [the longest x1 135 us: body(): pl.pallas_call(functools.partial(chain_kernel, float(count)), out_shape=(...]
    ppermute x110 -> x0, waiting for transfers between devices: 150 us -> none  [the longest x54 94.2 us: partner(): return lax.ppermute(block, axis, route)]
    psum x1 -> x0, blocking collectives: 82.6 us -> none  [body(): loss_sum, grad_head = lax.psum((loss_part, head_part), ('section', 'slab'))]
    transpose x9 -> x0, matrix products: 75 us -> none  [weight_grad(): return jnp.transpose(result, (2, 3, 4, 0, 1))]
    psum x1 -> x0, waiting for transfers between devices: 68 us -> none  [body(): grad_kernel, grad_mixing = lax.psum((loop_state[2], loop_state[3]), 'slab')]
    conv_general_dilated x18 -> x0, matrix products: 30.4 us -> none  [conv_local(): lax.conv_general_dilated(padded[None], kernel, (1, 1, 1), ((0, 0), (1, 1)...]
    dynamic_update_slice x45 -> x0, other arithmetic: 24 us -> none  [put_slot(): lax.dynamic_update_index_in_dim(buffer, jnp.where(active, value, previous...]
  transfers between devices with their start and end apart: 111 -> 0, of which waited for: 64 -> 0; matrix products, arithmetic and copies ran while one was open for 14% -> 0% of each run, Pallas kernels for 0% -> 0%
where the time goes in v1:
time: 164 us; the launch traced here: 163 us
  Pallas kernels  152 us (93%)
  local copies, waits for them, and re-layouts  7.06 us (4%)
  between operations  2.51 us (2%)
    pallas_call x1, Pallas kernels, body(): pl.pallas_call(functools.partial(chain_kernel, float(count)), out_shape=(...  135 us
    pallas_call x1, Pallas kernels, body(): pl.pallas_call(grads_kernel, grid=(3, 3), out_shape=(jax.ShapeDtypeStruct...  17.4 us
    unnamed x7, local copies, waits for them, and re-layouts  4.63 us

profile of v1, /device:TPU:1, one launch (start us, length us, event | category | flops | bytes accessed | tf_op | source)
XLA Modules:
  0.0 163.2 jit_solution(1359618019736359147)
XLA Ops:
  0.6 0.0 copy-start.1
  0.6 0.7 convert_bitcast_fusion.1
  1.4 0.1 pad.16
  1.4 0.8 copy.19
  2.2 0.1 reshape.34
  2.3 0.1 maximum_bitcast_fusion.1
  2.4 0.1 copy.15
  2.5 0.1 copy.16
  2.6 0.7 pad_bitcast_fusion.head_t
  3.3 0.8 copy.23
  4.1 1.0 copy.21
  5.2 0.1 pad.17.clone
  5.3 0.1 fusion
  5.4 0.3 maximum_bitcast_fusion
  5.8 0.1 bitcast_select_fusion.pay
  5.9 0.0 copy-done.1
  6.0 0.0 copy-start
  6.0 2.0 %copy-done = bf16[1,3,3,3,256,256]{5,4,3,2,1,0:T(8,128)(2,1)S(1)} copy-done((bf16[1,3,3,3,256,256]{5,4,3,2,1,0:T(8,128)(2,1)S(1)}, bf16[1,3,3,3,256,256]{5,4,3,2,1,0:T(8,128)(2,1)}, u32[]{:S(2)}) %copy-start) | copy-done | bytes 3538968
  8.0 134.9 %chain.1 = (bf16[2,8,2,2,64,256]{5,4,3,2,1,0:T(8,128)(2,1)S(1)}, bf16[2,8,2,2,64,256]{5,4,3,2,1,0:T(8,128)(2,1)S(1)}, bf16[2,8,2,2,64,256]{5,4,3,2,1,0:T(8,128)(2,1)S(1)}, f32[8,256]{1,0:T(8,128)S(1)}) custom-call(bf16[16,2,16,256]{3,2,1,0:T(8,128)(2,1)S(1)} %bitcast_select_fusion.pay, bf16[3,3,3,256,256]{4,3,2,1,0:T(8,128)(2,1)S(1)} %bitcast.26, ...), custom_call_target="tpu_custom_call" | custom-call | tf_op jit(solution)/shard_map/chain/pallas_call | solution.py:560
  142.9 0.5 slice.22
  144.1 0.6 slice_bitcast_fusion
  144.6 17.4 %grads.1 = (f32[3,3,3,256,256]{4,3,2,1,0:T(8,128)}, f32[256,256]{1,0:T(8,128)}) custom-call(bf16[2,8,2,2,64,256]{5,4,3,2,1,0:T(8,128)(2,1)S(1)} %get-tuple-element.11.xg, bf16[2,8,2,2,64,256]{5,4,3,2,1,0:T(8,128)(2,1)S(1)} %get-tuple-element.12.bg, bf16[2,8,2,2,64,256]{5,4,3,2,1,0:T(8,128)(2,1)S(1)} %get-tuple-element.13.pg), custom_call_target="tpu_custom_call" | custom-call | tf_op jit(solution)/shard_map/grads/pallas_call | solution.py:589
  (4 shorter events, 0.0 us)
Async XLA Ops:
  0.6 5.3 %copy-start.1 = (bf16[1,256,256]{2,1,0:T(8,128)(2,1)S(1)}, bf16[1,256,256]{2,1,0:T(8,128)(2,1)}, u32[]{:S(2)}) copy-start(bf16[1,256,256]{2,1,0:T(8,128)(2,1)} %param.10) | copy-start | bytes 393220
  6.0 2.0 %copy-start = (bf16[1,3,3,3,256,256]{5,4,3,2,1,0:T(8,128)(2,1)S(1)}, bf16[1,3,3,3,256,256]{5,4,3,2,1,0:T(8,128)(2,1)}, u32[]{:S(2)}) copy-start(bf16[1,3,3,3,256,256]{5,4,3,2,1,0:T(8,128)(2,1)} %param.9) | copy-start | bytes 10616836

commit v2 on v1

v2 whole, which is shorter than its diff:
```python
import functools

import jax
import jax.numpy as jnp
from jax import lax
from jax.experimental import pallas as pl
from jax.experimental.pallas import tpu as pltpu
from jax.sharding import PartitionSpec as P

loss_scale = 1024.0
MESH = pl.DeviceIdType.MESH
F32 = jnp.float32
BF16 = jnp.bfloat16


STAGE, LABELS, HEADS, SUMS, INPUTS, BRANCHES, GRADS, TWIN = 0, 1, 2, 3, 4, 5, 6, 4
BASE, STRIDE = 12, 14
MAIN, MIRROR, SLOPE, DOWN, SKIP, EDGE = 0, 3, 4, 6, 9, 12
GREETED = 28


def dot(a, b):
    return jnp.dot(a, b, preferred_element_type=F32)


def dot_nt(a, b):
    return lax.dot_general(a, b, (((1,), (1,)), ((), ())), preferred_element_type=F32)


def shifted(value, by):
    rows = value.shape[0]
    depth = lax.broadcasted_iota(jnp.int32, value.shape, 0) & 15
    rolled = pltpu.roll(value, (rows - by) % rows, 0)
    inside = depth < 15 if by > 0 else depth > 0
    return jnp.where(inside, rolled, 0.0)


def logistic(value):
    return 1.0 / (1.0 + jnp.exp(-value))


def spread_grads(pg, pgs):
    def turn(step, carry):
        for r in range(2):
            both = jnp.concatenate([pg[0, step, r], pg[1, step, r]], axis=0)
            wide = both.astype(F32)
            rows = pl.ds(pl.multiple_of(16 + step * 128, 16), 128)
            pgs[0, r, rows, :] = shifted(wide, 1).astype(BF16)
            pgs[1, r, rows, :] = both
            pgs[2, r, rows, :] = shifted(wide, -1).astype(BF16)
        return carry

    lax.fori_loop(0, 8, turn, 0)
    for k in range(3):
        for r in range(2):
            pgs[k, r, 0:16, :] = jnp.zeros((16, 256), BF16)
            pgs[k, r, 1040:1056, :] = jnp.zeros((16, 256), BF16)


def tap_grads(xt, pgs, kd, kc):
    rows = pl.ds(pl.multiple_of((2 - kc) * 16, 16), 1024)
    first = dot(xt[...], pgs[kd, 0, rows, :])
    second = dot(xt[...], pgs[kd, 1, rows, :])
    return second[:256], first[:256] + second[256:], first[256:]


def mix_grad(bt, pgs):
    return dot(bt[0:256], pgs[1, 0, 16:1040, :]) + dot(bt[256:512], pgs[1, 1, 16:1040, :])


def chain_kernel(
    count,
    fx_hbm,
    lab_hbm,
    offsets_hbm,
    weight_hbm,
    mixing_hbm,
    head_hbm,
    xt,
    bt,
    pg,
    acc,
    acc_mix,
    sums,
    fx,
    lab,
    offsets,
    weight,
    mixing,
    head_in,
    turned,
    head,
    pay,
    stage,
    xg,
    bg,
    pgs,
    xc,
    bc,
    ys,
    slope,
    cot,
    laball,
    labs,
    down_in,
    down_out,
    skip_in,
    skip_out,
    pgc,
    heads,
    total,
    ssem,
    rsem,
    wsem,
):
    sec = lax.axis_index("section")
    me = lax.axis_index("slab")
    chip = me // 2
    core = me % 2

    loads = [
        pltpu.make_async_copy(src, dst, wsem.at[k])
        for k, (src, dst) in enumerate(
            (
                (fx_hbm, fx),
                (lab_hbm, lab),
                (head_hbm, head_in),
                (mixing_hbm, mixing),
                (offsets_hbm, offsets),
                (weight_hbm, weight),
            )
        )
    ]
    for load in loads:
        load.start()

    barrier = pltpu.get_barrier_semaphore()

    def greet(s, d):
        pl.semaphore_signal(barrier, inc=1, device_id=(s, d), device_id_type=MESH)

    def greet_section(step, carry):
        greet(sec, (me + step) % 16)
        return carry

    def greet_column(step, carry):
        greet((sec + step) % 8, me)
        return carry

    lax.fori_loop(1, 16, greet_section, 0)
    lax.fori_loop(1, 8, greet_column, 0)
    for b in (1, 15):
        for a in (1, 7):
            greet((sec + a) % 8, (me + b) % 16)
        greet(7 - sec, (me + b) % 16)

    def remote(src, dst, index, device):
        return pltpu.make_async_remote_copy(
            src_ref=src,
            dst_ref=dst,
            send_sem=ssem.at[index],
            recv_sem=rsem.at[index],
            device_id=device,
            device_id_type=MESH,
        )

    has_left = me > 0
    has_right = me < 15
    to_left = jnp.maximum(me - 1, 0)
    to_right = jnp.minimum(me + 1, 15)
    above = jnp.minimum(sec + 1, 7)
    below = jnp.maximum(sec - 1, 0)

    def with_halos(src, dst, index, other, first):
        return (
            remote(
                src.at[:, pl.ds(first, 64)], dst.at[:, pl.ds(16, 64)], index, (other, me)
            ),
            remote(
                src.at[:, pl.ds(first, 16)],
                dst.at[:, pl.ds(80, 16)],
                index + 1,
                (other, to_left),
            ),
            remote(
                src.at[:, pl.ds(first + 48, 16)],
                dst.at[:, pl.ds(0, 16)],
                index + 2,
                (other, to_right),
            ),
        )

    def edges(ref, index):
        return (
            remote(
                ref.at[:, pl.ds(16, 16)], ref.at[:, pl.ds(80, 16)], index, (sec, to_left)
            ),
            remote(
                ref.at[:, pl.ds(64, 16)], ref.at[:, pl.ds(0, 16)], index + 1, (sec, to_right)
            ),
        )

    def start_sides(left, right):
        @pl.when(has_left)
        def _():
            left.start()

        @pl.when(has_right)
        def _():
            right.start()

    def sent_sides(left, right):
        @pl.when(has_left)
        def _():
            left.wait_send()

        @pl.when(has_right)
        def _():
            right.wait_send()

    def got_sides(left, right):
        @pl.when(has_right)
        def _():
            left.wait_recv()

        @pl.when(has_left)
        def _():
            right.wait_recv()

    def stage_copy(peer):
        return remote(pay.at[peer], stage.at[me], STAGE, (sec, peer))

    def label_copy(peer):
        return remote(laball.at[me], laball.at[me], LABELS, (sec, peer))

    for load in loads[:3]:
        load.wait()

    @pl.when(sec == 0)
    def _():
        out_row = lax.broadcasted_iota(jnp.int32, (256, 128), 0)
        cell = lax.broadcasted_iota(jnp.int32, (256, 128), 1)
        wanted = 4 * (out_row >> 4) - 2 + (out_row & 7)
        same = ((cell & 63) == wanted) & ((cell >> 6) == ((out_row >> 3) & 1))
        pick = jnp.where(same, 1.0, 0.0).astype(BF16)
        for m in range(2):
            pay[:, m] = dot(pick, fx[m]).astype(BF16).reshape(16, 16, 256)
        stage[me] = pay[me]

    @pl.when(sec == 7)
    def _():
        laball[me] = jnp.zeros((8, 128), F32)
        for m in range(2):
            laball[me, 2 * m : 2 * m + 2, 0:64] = lab[m].astype(F32)

    head[...] = jnp.zeros((128, 256), BF16)
    head[0:16, :] = jnp.concatenate(
        [head_in[...].astype(F32), jnp.zeros((13, 256), F32)], axis=0
    ).astype(BF16)

    def clear(rows):
        nothing = jnp.zeros((2, 2, 16, 256), BF16)
        for ref in (xc, pgc, down_in, skip_in):
            ref[:, :, rows, :] = nothing
        slope[:, :, rows, :] = jnp.zeros((2, 2, 16, 256), F32)

    @pl.when(me == 0)
    def _():
        clear(slice(0, 16))

    @pl.when(me == 15)
    def _():
        clear(slice(80, 96))

    pl.semaphore_wait(barrier, GREETED)

    @pl.when(sec == 0)
    def _():
        def send(step, carry):
            stage_copy((me + step) % 16).start()
            return carry

        lax.fori_loop(1, 16, send, 0)

    @pl.when(sec == 7)
    def _():
        def send(step, carry):
            label_copy((me + step) % 16).start()
            return carry

        lax.fori_loop(1, 16, send, 0)

    for load in loads[3:]:
        load.wait()

    def turn_weights():
        def turn(k, carry):
            a, b, c = k // 9, k // 3 % 3, k % 3
            turned[a, b, c] = weight[a, b, c].T
            return carry

        lax.fori_loop(0, 27, turn, 0)

    @pl.when(sec >= 1)
    def _():
        turn_weights()

    @pl.when(sec == 0)
    def _():
        all_staged = remote(stage.at[pl.ds(0, 15)], stage.at[pl.ds(0, 15)], STAGE, (sec, to_left))
        all_staged.wait_recv()
        out_row = lax.broadcasted_iota(jnp.int32, (192, 256), 0)
        in_row = lax.broadcasted_iota(jnp.int32, (192, 256), 1)
        second = (out_row >= 96).astype(jnp.int32)
        rest = out_row - 96 * second
        wanted = (rest & 15) * 16 + second * 8 + (rest >> 4) + 1
        pick = jnp.where(in_row == wanted, 1.0, 0.0).astype(BF16)
        for m in range(2):
            xc[m] = dot(pick, stage[:, m].reshape(256, 256)).astype(BF16).reshape(2, 96, 256)
        all_staged.wait_send()

    @pl.when(sec == 7)
    def _():
        labeled = remote(laball.at[pl.ds(0, 15)], laball.at[pl.ds(0, 15)], LABELS, (sec, to_left))
        labeled.wait_send()
        labeled.wait_recv()
        known = laball[...].reshape(128, 128).astype(BF16)
        out_row = lax.broadcasted_iota(jnp.int32, (192, 128), 0)
        lane = lax.broadcasted_iota(jnp.int32, (192, 128), 1)
        second = (out_row >= 96).astype(jnp.int32)
        rest = out_row - 96 * second
        for m in range(2):
            pick = jnp.where(lane == (rest & 15) * 8 + 2 * m + second, 1.0, 0.0).astype(BF16)
            row = dot(pick, known)
            here = jnp.where(lane == 4 * me - 1 + (rest >> 4), row, 0.0)
            labs[m] = jnp.broadcast_to(jnp.sum(here, axis=1, keepdims=True), (192, 128))

    def gather(out, index):
        def to_peer(peer):
            block = out.at[core, chip]
            return remote(block, block, index, (sec, peer * 2 + core))

        def send(step, carry):
            to_peer((chip + step) % 8).start()
            return carry

        lax.fori_loop(1, 8, send, 0)

    def gather_twin(out, index):
        seven = out.at[core, pl.ds(0, 7)]
        peers = remote(seven, seven, index, (sec, (chip + 1) % 8 * 2 + core))
        peers.wait_send()
        peers.wait_recv()
        remote(out.at[core], out.at[core], index + TWIN, (sec, chip * 2 + 1 - core)).start()

    def gather_end(out, index):
        twin = remote(out.at[core], out.at[core], index + TWIN, (sec, chip * 2 + 1 - core))
        twin.wait_send()
        twin.wait_recv()

    def forward_copies(m):
        base = BASE + STRIDE * m
        main, left, right = with_halos(ys.at[m], xc.at[m], base + MAIN, above, 0)
        mirror = remote(ys.at[m], bc.at[m], base + MIRROR, (7 - sec, me))
        return main, left, right, mirror

    def loss_and_cotangent(m, output):
        logits = dot_nt(output, head[...])
        label = labs[m]
        lane = lax.broadcasted_iota(jnp.int32, (1, 128), 1)

        def by_channel(k):
            return jnp.where(
                lane == 0, offsets[0, k], jnp.where(lane == 1, offsets[1, k], offsets[2, k])
            )

        along_depth, along_row, along_col = by_channel(0), by_channel(1), by_channel(2)
        near = jnp.where(
            along_depth < 0,
            shifted(label, -1),
            jnp.where(along_depth > 0, shifted(label, 1), label),
        )
        rows = []
        for r in range(2):
            start = 96 * r
            rows.append(
                jnp.where(
                    along_col < 0,
                    near[start : start + 64],
                    jnp.where(
                        along_col > 0, near[start + 32 : start + 96], near[start + 16 : start + 80]
                    ),
                )
            )
        zero = jnp.zeros((64, 128), F32)
        first = jnp.where(along_row < 0, zero, jnp.where(along_row > 0, rows[1], rows[0]))
        second = jnp.where(along_row > 0, zero, jnp.where(along_row < 0, rows[0], rows[1]))
        neighbor = jnp.concatenate([first, second], axis=0)
        own = jnp.concatenate([label[16:80], label[112:176]], axis=0)
        target = jnp.where((neighbor == own) & (own != 0.0), 1.0, 0.0)
        channel = lax.broadcasted_iota(jnp.int32, (128, 128), 1) < 3
        soft = jnp.maximum(logits, 0.0) + jnp.log1p(jnp.exp(-jnp.abs(logits)))
        loss = jnp.sum(jnp.where(channel, soft - target * logits, 0.0))
        grad = jnp.where(channel, loss_scale * (logistic(logits) - target) / count, 0.0)
        rounded = grad.astype(BF16)
        cot[m] = dot(rounded, head[...])
        across = rounded.astype(F32).T.astype(BF16)
        grad_head = dot(across, output)[0:8]
        row = lax.broadcasted_iota(jnp.int32, (8, 256), 0)
        partial = jnp.where(row == 3, loss, grad_head)

        @pl.when(m == 0)
        def _():
            heads[me] = partial

        @pl.when(m > 0)
        def _():
            heads[me] = heads[me] + partial

    def forward(m, carry):
        main, left, right, mirror = forward_copies(m)

        @pl.when(sec > 0)
        def _():
            main.wait_recv()
            got_sides(left, right)

        @pl.when(sec <= 4)
        def _():
            bc[m] = xc[m, :, 16:80, :]

        parts = []
        for kd in range(3):
            same = top = bottom = None
            for kc in range(3):
                both = xc[m, :, 16 * kc : 16 * kc + 64, :]
                part = dot(both.reshape(128, 256), weight[kd, 1, kc])
                high = dot(both[1], weight[kd, 2, kc])
                low = dot(both[0], weight[kd, 0, kc])
                same = part if same is None else same + part
                top = high if top is None else top + high
                bottom = low if bottom is None else bottom + low
            parts.append(same + jnp.concatenate([top, bottom], axis=0))

        preact = parts[1] + shifted(parts[0], -1) + shifted(parts[2], 1)
        preact = preact + dot(bc[m].reshape(128, 256), mixing[...])
        sigma = logistic(preact)
        output = (preact / (1.0 + jnp.exp(-preact))).astype(BF16)
        ys[m] = output.reshape(2, 64, 256)

        @pl.when(sec < 7)
        def _():
            start_sides(left, right)
            main.start()

        @pl.when(sec < 3)
        def _():
            mirror.start()

        slope[m, :, 16:80, :] = (sigma * (1.0 + preact * (1.0 - sigma))).reshape(2, 64, 256)

        @pl.when((sec > 0) & (sec < 7))
        def _():
            start_sides(*edges(slope.at[m], BASE + STRIDE * m + SLOPE))

        @pl.when(sec == 7)
        def _():
            loss_and_cotangent(m, output)

        return carry

    @pl.when(sec >= 5)
    def _():
        for m in range(2):
            forward_copies(m)[3].wait_recv()
            bg[core, chip, m] = bc[m]
        gather(bg, BRANCHES)

    lax.fori_loop(0, 2, forward, 0)

    def gather_inputs():
        for m in range(2):
            xg[core, chip, m] = xc[m, :, 16:80, :]
        gather(xg, INPUTS)
        gather_twin(xg, INPUTS)

        @pl.when(sec >= 5)
        def _():
            gather_end(bg, BRANCHES)

        gather_end(xg, INPUTS)

        def turn(step, carry):
            lanes = pl.ds(pl.multiple_of(step * 128, 128), 128)
            for m in range(2):
                for r in range(2):
                    block = jnp.concatenate([xg[0, step, m, r], xg[1, step, m, r]], axis=0)
                    flipped = block.T
                    xt[m, 256 * r : 256 * r + 256, lanes] = flipped

                    @pl.when(sec < 5)
                    def _():
                        bt[m, 256 * r : 256 * r + 256, lanes] = flipped

                    @pl.when(sec >= 5)
                    def _():
                        other = jnp.concatenate([bg[0, step, m, r], bg[1, step, m, r]], axis=0)
                        bt[m, 256 * r : 256 * r + 256, lanes] = other.T

            return carry

        lax.fori_loop(0, 8, turn, 0)

    @pl.when(sec >= 5)
    def _():
        gather_twin(bg, BRANCHES)

    @pl.when(sec < 6)
    def _():
        gather_inputs()

    def backward_copies(m):
        base = BASE + STRIDE * m
        down = with_halos(down_out.at[m], down_in.at[m], base + DOWN, below, 0)
        skip = with_halos(skip_out.at[m], skip_in.at[m], base + SKIP, 7 - sec, 0)
        return down, skip, edges(pgc.at[m], base + EDGE)

    def gather_grads(m):
        pg[m, core, chip] = pgc[m, :, 16:80, :]
        gather(pg.at[m], GRADS + m)

    def backward(m, carry):
        down, skip, edge = backward_copies(m)

        @pl.when(sec == 7)
        def _():
            grad = cot[m].reshape(2, 64, 256) * slope[m, :, 16:80, :]
            pgc[m, :, 16:80, :] = grad.astype(BF16)
            start_sides(*edge)
            got_sides(*edge)

        @pl.when(sec == 0)
        def _():
            down[0].wait_recv()
            skip[0].wait_recv()
            upstream = down_in[m, :, 16:80, :].astype(F32) + skip_in[m, :, 16:80, :].astype(F32)
            pgc[m, :, 16:80, :] = (upstream * slope[m, :, 16:80, :]).astype(BF16)
            gather_grads(m)

        @pl.when((sec > 0) & (sec < 7))
        def _():
            @pl.when(sec < 4)
            def _():
                skip[0].wait_recv()
                got_sides(*skip[1:])

            down[0].wait_recv()
            got_sides(*down[1:])
            got_sides(*edges(slope.at[m], BASE + STRIDE * m + SLOPE))
            upstream = down_in[m].astype(F32)
            mirrored = jnp.where(sec < 4, skip_in[m].astype(F32), 0.0)
            pgc[m] = ((upstream + mirrored) * slope[m]).astype(BF16)

        @pl.when(sec > 0)
        def _():
            branch = dot_nt(pgc[m, :, 16:80, :].reshape(128, 256), mixing[...])

            @pl.when(sec >= 4)
            def _():
                skip_out[m] = branch.astype(BF16).reshape(2, 64, 256)
                skip[0].start()

                @pl.when(sec < 7)
                def _():
                    start_sides(*skip[1:])

            parts = []
            for kd in range(3):
                same = top = bottom = None
                for kc in range(3):
                    both = pgc[m, :, 16 * (2 - kc) : 16 * (2 - kc) + 64, :]
                    part = dot(both.reshape(128, 256), turned[kd, 1, kc])
                    high = dot(both[1], turned[kd, 0, kc])
                    low = dot(both[0], turned[kd, 2, kc])
                    same = part if same is None else same + part
                    top = high if top is None else top + high
                    bottom = low if bottom is None else bottom + low
                parts.append(same + jnp.concatenate([top, bottom], axis=0))
            result = parts[1] + shifted(parts[0], 1) + shifted(parts[2], -1)
            result = jnp.where(sec < 4, result + branch, result)
            down_out[m] = result.astype(BF16).reshape(2, 64, 256)

            @pl.when(sec > 1)
            def _():
                start_sides(*down[1:])

            down[0].start()

        return carry

    lax.fori_loop(0, 2, backward, 0)

    @pl.when(sec > 0)
    def _():
        for m in range(2):
            gather_grads(m)

    def head_copy(peer):
        return remote(heads.at[me], heads.at[me], HEADS, (7, peer))

    def sum_copy(other):
        return remote(total, sums, SUMS, (other, me))

    @pl.when(sec == 7)
    def _():
        def send(step, carry):
            head_copy((me + step) % 16).start()
            return carry

        lax.fori_loop(1, 16, send, 0)
        all_heads = remote(heads.at[pl.ds(0, 15)], heads.at[pl.ds(0, 15)], HEADS, (7, to_left))
        all_heads.wait_send()
        all_heads.wait_recv()
        whole = heads[0]
        for k in range(1, 16):
            whole = whole + heads[k]
        total[...] = whole
        sums[...] = whole

        def spread(other, carry):
            sum_copy(other).start()
            return carry

        lax.fori_loop(0, 7, spread, 0)

    @pl.when(sec >= 6)
    def _():
        gather_inputs()

    gather_twin(pg.at[0], GRADS)
    gather_end(pg.at[0], GRADS)
    spread_grads(pg.at[0], pgs)
    acc_mix[...] = mix_grad(bt.at[0], pgs)

    def taps(k, carry):
        kd, kc = k // 3, k % 3

        @pl.when(k == 4)
        def _():
            gather_twin(pg.at[1], GRADS + 1)

        found = tap_grads(xt.at[0], pgs, kd, kc)
        for kr in range(3):
            acc[kd, kr, kc] = found[kr]
        return carry

    lax.fori_loop(0, 9, taps, 0)
    gather_end(pg.at[1], GRADS + 1)

    @pl.when(sec == 7)
    def _():
        def ended(other, carry):
            sum_copy(other).wait_send()
            return carry

        lax.fori_loop(0, 7, ended, 0)

    @pl.when(sec < 7)
    def _():
        sum_copy(7).wait_recv()

    def finish(m, carry):
        main, left, right, mirror = forward_copies(m)
        down, skip, edge = backward_copies(m)

        @pl.when(sec < 7)
        def _():
            main.wait_send()
            sent_sides(left, right)

        @pl.when(sec < 3)
        def _():
            mirror.wait_send()

        @pl.when((sec > 0) & (sec < 7))
        def _():
            sent_sides(*edges(slope.at[m], BASE + STRIDE * m + SLOPE))

        @pl.when(sec > 0)
        def _():
            down[0].wait_send()

        @pl.when(sec > 1)
        def _():
            sent_sides(*down[1:])

        @pl.when(sec >= 4)
        def _():
            skip[0].wait_send()

            @pl.when(sec < 7)
            def _():
                sent_sides(*skip[1:])

        @pl.when(sec == 7)
        def _():
            sent_sides(*edge)

        return carry

    lax.fori_loop(0, 2, finish, 0)


def grads_kernel(count, xt, bt, pg, acc, acc_mix, sums, out, out_mix, out_head, out_loss, pgs):
    kd = pl.program_id(0)
    kc = pl.program_id(1)

    @pl.when((kd == 0) & (kc == 0))
    def _():
        spread_grads(pg.at[1], pgs)
        out_mix[...] = acc_mix[...] + mix_grad(bt.at[1], pgs)
        out_head[...] = sums[0:3, :]
        out_loss[...] = sums[3:4, 0:1] / count

    found = tap_grads(xt.at[1], pgs, kd, kc)
    for kr in range(3):
        out[0, kr, 0] = acc[kd, kr, kc] + found[kr]


def body(features_in, labels, offsets, conv_weight, branch_weight, head_weight):
    micro, channels = features_in.shape[0], features_in.shape[1]
    outs = offsets.shape[0]
    rows, columns = features_in.shape[3], features_in.shape[4]
    cells = features_in.shape[2] * rows * columns
    count = float(micro * outs * cells * lax.axis_size("slab"))
    features = jnp.transpose(features_in[:, :, 0], (0, 2, 3, 1)).reshape(2, 128, channels)
    vmem = pl.BlockSpec(memory_space=pltpu.VMEM)
    hbm = pl.BlockSpec(memory_space=pltpu.HBM)
    gathered = (2, 8, micro, 2, 64, channels)
    block = (micro, 2, 64, channels)
    wide = (micro, 2, 96, channels)
    kernel_shape = (3, 3, 3, channels, channels)
    semaphores = BASE + STRIDE * micro
    middle = pl.pallas_call(
        functools.partial(chain_kernel, count),
        out_shape=(
            jax.ShapeDtypeStruct((micro, 512, 1024), BF16),
            jax.ShapeDtypeStruct((micro, 512, 1024), BF16),
            jax.ShapeDtypeStruct((micro, 2, 8, 2, 64, channels), BF16),
            jax.ShapeDtypeStruct(kernel_shape, F32),
            jax.ShapeDtypeStruct((channels, channels), F32),
            jax.ShapeDtypeStruct((8, channels), F32),
        ),
        in_specs=[hbm] * 6,
        out_specs=(vmem,) * 6,
        scratch_shapes=[
            pltpu.VMEM((micro, 128, channels), BF16),
            pltpu.VMEM((micro, rows, columns), jnp.int32),
            pltpu.SMEM((outs, 3), jnp.int32),
            pltpu.VMEM(kernel_shape, BF16),
            pltpu.VMEM((channels, channels), BF16),
            pltpu.VMEM((outs, channels), BF16),
            pltpu.VMEM(kernel_shape, BF16),
            pltpu.VMEM((128, channels), BF16),
            pltpu.VMEM((16, micro, 16, channels), BF16),
            pltpu.VMEM((16, micro, 16, channels), BF16),
            pltpu.VMEM(gathered, BF16),
            pltpu.VMEM(gathered, BF16),
            pltpu.VMEM((3, 2, 1056, channels), BF16),
            pltpu.VMEM(wide, BF16),
            pltpu.VMEM(block, BF16),
            pltpu.VMEM(block, BF16),
            pltpu.VMEM(wide, F32),
            pltpu.VMEM((micro, 128, channels), F32),
            pltpu.VMEM((16, 8, 128), F32),
            pltpu.VMEM((micro, 192, 128), F32),
            pltpu.VMEM(wide, BF16),
            pltpu.VMEM(block, BF16),
            pltpu.VMEM(wide, BF16),
            pltpu.VMEM(block, BF16),
            pltpu.VMEM(wide, BF16),
            pltpu.VMEM((16, 8, channels), F32),
            pltpu.VMEM((8, channels), F32),
            pltpu.SemaphoreType.DMA((semaphores,)),
            pltpu.SemaphoreType.DMA((semaphores,)),
            pltpu.SemaphoreType.DMA((6,)),
        ],
        compiler_params=pltpu.CompilerParams(
            collective_id=0, has_side_effects=True, vmem_limit_bytes=34 * 1024 * 1024
        ),
        name="chain",
    )(
        *(
            pltpu.with_memory_space_constraint(value, pltpu.HBM)
            for value in (
                features,
                labels.reshape(micro, rows, columns),
                offsets,
                conv_weight[0],
                branch_weight[0],
                head_weight.T,
            )
        )
    )

    grad_kernel, grad_mixing, grad_head, loss = pl.pallas_call(
        functools.partial(grads_kernel, count),
        grid=(3, 3),
        out_shape=(
            jax.ShapeDtypeStruct(kernel_shape, F32),
            jax.ShapeDtypeStruct((channels, channels), F32),
            jax.ShapeDtypeStruct((outs, channels), F32),
            jax.ShapeDtypeStruct((1, 1), F32),
        ),
        in_specs=[vmem] * 6,
        out_specs=(
            pl.BlockSpec((1, 3, 1, channels, channels), lambda kd, kc: (kd, 0, kc, 0, 0)),
            pl.BlockSpec((channels, channels), lambda kd, kc: (0, 0)),
            pl.BlockSpec((outs, channels), lambda kd, kc: (0, 0)),
            pl.BlockSpec((1, 1), lambda kd, kc: (0, 0)),
        ),
        scratch_shapes=[pltpu.VMEM((3, 2, 1056, channels), BF16)],
        compiler_params=pltpu.CompilerParams(vmem_limit_bytes=32 * 1024 * 1024),
        name="grads",
    )(*middle)
    return (loss.reshape(()), grad_kernel[None], grad_mixing[None], grad_head.T)


def solution(mesh):
    placed = (
        P(None, None, "slab", None, None),
        P(None, "slab", None, None),
        P(),
        P("section", None, None, None, None, None),
        P("section", None, None),
        P(),
    )
    return jax.shard_map(
        body,
        mesh=mesh,
        in_specs=placed,
        out_specs=(P(), P("section", None, None, None, None, None), P("section", None, None), P()),
        check_vma=False,
    )
```

time: 164 us -> 134 us (0.82)
  the two profiles are of different devices: /device:TPU:1 before, /device:TPU:45 now
where the time goes in v2:
time: 134 us
  Pallas kernels  134 us (100%)
    pallas_call x1, Pallas kernels, body(): pl.pallas_call(functools.partial(chain_kernel, count), out_shape=(jax.Sha...  124 us
    pallas_call x1, Pallas kernels, body(): pl.pallas_call(functools.partial(grads_kernel, count), grid=(3, 3), out_s...  9.21 us

profile of v2, /device:TPU:45, one launch (start us, length us, event | category | flops | bytes accessed | tf_op | source)
XLA Modules:
  0.0 134.2 jit_solution(9597298961902434391)
XLA Ops:
  0.6 124.4 %chain.1 = (bf16[2,512,1024]{2,1,0:T(8,128)(2,1)S(1)}, bf16[2,512,1024]{2,1,0:T(8,128)(2,1)S(1)}, bf16[2,2,8,2,64,256]{5,4,3,2,1,0:T(8,128)(2,1)S(1)}, f32[3,3,3...) custom-call(bf16[2,128,256]{2,1,0:T(8,128)(2,1)} %bitcast.14, s32[2,2,64]{2,1,0:T(2,128)} %bitcast.16, ...), custom_call_target="tpu_custom_call" | custom-call | tf_op jit(solution)/shard_map/chain/pallas_call | solution.py:744
  125.0 9.2 %grads.1 = (f32[3,3,3,256,256]{4,3,2,1,0:T(8,128)}, f32[256,256]{1,0:T(8,128)}, f32[3,256]{1,0:T(4,128)}, f32[1,1]{1,0:T(1,128)}) custom-call(bf16[2,512,1024]{2,1,0:T(8,128)(2,1)S(1)} %get-tuple-element.14.xt, bf16[2,512,1024]{2,1,0:T(8,128)(2,1)S(1)} %get-tuple-element.15.bt, bf16[2,2,8,2,64,256]{5,4,3,2,1,0:T(8,128)(2,1)S(1)} %get-tuple-element.16.pg, ...), custom_call_target="tpu_custom_call" | custom-call | tf_op jit(solution)/shard_map/grads/pallas_call | solution.py:806

commit v3 on v2

--- a/solution.py
+++ b/solution.py
@@ -14,6 +14,7 @@
 
 
 STAGE, LABELS, HEADS, SUMS, INPUTS, BRANCHES, GRADS, TWIN = 0, 1, 2, 3, 4, 5, 6, 4
+TAPS, MIXED = 10, 11
 BASE, STRIDE = 12, 14
 MAIN, MIRROR, SLOPE, DOWN, SKIP, EDGE = 0, 3, 4, 6, 9, 12
 GREETED = 28
@@ -39,33 +40,22 @@
     return 1.0 / (1.0 + jnp.exp(-value))
 
 
-def spread_grads(pg, pgs):
+def spread_grads(found, pgs):
     def turn(step, carry):
+        rows = pl.ds(pl.multiple_of(16 + step * 128, 16), 128)
         for r in range(2):
-            both = jnp.concatenate([pg[0, step, r], pg[1, step, r]], axis=0)
+            lanes = slice(128 * r, 128 * r + 128)
+            both = jnp.concatenate([found[2 * step, r], found[2 * step + 1, r]], axis=0)
             wide = both.astype(F32)
-            rows = pl.ds(pl.multiple_of(16 + step * 128, 16), 128)
-            pgs[0, r, rows, :] = shifted(wide, 1).astype(BF16)
-            pgs[1, r, rows, :] = both
-            pgs[2, r, rows, :] = shifted(wide, -1).astype(BF16)
+            pgs[0, rows, lanes] = shifted(wide, 1).astype(BF16)
+            pgs[1, rows, lanes] = both
+            pgs[2, rows, lanes] = shifted(wide, -1).astype(BF16)
         return carry
 
     lax.fori_loop(0, 8, turn, 0)
     for k in range(3):
-        for r in range(2):
-            pgs[k, r, 0:16, :] = jnp.zeros((16, 256), BF16)
-            pgs[k, r, 1040:1056, :] = jnp.zeros((16, 256), BF16)
-
-
-def tap_grads(xt, pgs, kd, kc):
-    rows = pl.ds(pl.multiple_of((2 - kc) * 16, 16), 1024)
-    first = dot(xt[...], pgs[kd, 0, rows, :])
-    second = dot(xt[...], pgs[kd, 1, rows, :])
-    return second[:256], first[:256] + second[256:], first[256:]
-
-
-def mix_grad(bt, pgs):
-    return dot(bt[0:256], pgs[1, 0, 16:1040, :]) + dot(bt[256:512], pgs[1, 1, 16:1040, :])
+        pgs[k, 0:16, :] = jnp.zeros((16, 256), BF16)
+        pgs[k, 1040:1056, :] = jnp.zeros((16, 256), BF16)
 
 
 def chain_kernel(
@@ -76,12 +66,13 @@
     weight_hbm,
     mixing_hbm,
     head_hbm,
-    xt,
-    bt,
-    pg,
     acc,
     acc_mix,
     sums,
+    xt,
+    bt,
+    pgo,
+    pgh,
     fx,
     lab,
     offsets,
@@ -99,7 +90,6 @@
     bc,
     ys,
     slope,
-    cot,
     laball,
     labs,
     down_in,
@@ -112,6 +102,7 @@
     ssem,
     rsem,
     wsem,
+    token,
 ):
     sec = lax.axis_index("section")
     me = lax.axis_index("slab")
@@ -399,11 +390,13 @@
         own = jnp.concatenate([label[16:80], label[112:176]], axis=0)
         target = jnp.where((neighbor == own) & (own != 0.0), 1.0, 0.0)
         channel = lax.broadcasted_iota(jnp.int32, (128, 128), 1) < 3
+        grad = jnp.where(channel, loss_scale * (logistic(logits) - target) / count, 0.0)
+        rounded = grad.astype(BF16)
+        head_cot = dot(rounded, head[...]).reshape(2, 64, 256)
+        pgc[m, :, 16:80, :] = (head_cot * slope[m, :, 16:80, :]).astype(BF16)
+        start_sides(*edges(pgc.at[m], BASE + STRIDE * m + EDGE))
         soft = jnp.maximum(logits, 0.0) + jnp.log1p(jnp.exp(-jnp.abs(logits)))
         loss = jnp.sum(jnp.where(channel, soft - target * logits, 0.0))
-        grad = jnp.where(channel, loss_scale * (logistic(logits) - target) / count, 0.0)
-        rounded = grad.astype(BF16)
-        cot[m] = dot(rounded, head[...])
         across = rounded.astype(F32).T.astype(BF16)
         grad_head = dot(across, output)[0:8]
         row = lax.broadcasted_iota(jnp.int32, (8, 256), 0)
@@ -525,24 +518,33 @@
         skip = with_halos(skip_out.at[m], skip_in.at[m], base + SKIP, 7 - sec, 0)
         return down, skip, edges(pgc.at[m], base + EDGE)
 
+    def grad_copy(m, peer):
+        return remote(pgo.at[m, peer % 2], pgh.at[m, me], GRADS + m, (sec, peer))
+
     def gather_grads(m):
-        pg[m, core, chip] = pgc[m, :, 16:80, :]
-        gather(pg.at[m], GRADS + m)
+        block = pgc[m, :, 16:80, :]
+        low, high = block[:, :, :128], block[:, :, 128:]
+        pgo[m, 0] = low
+        pgo[m, 1] = high
+
+        def send(step, carry):
+            grad_copy(m, (me + step) % 16).start()
+            return carry
+
+        lax.fori_loop(1, 16, send, 0)
+        pgh[m, me] = pgo[m, core]
 
     def backward(m, carry):
         down, skip, edge = backward_copies(m)
 
         @pl.when(sec == 7)
         def _():
-            grad = cot[m].reshape(2, 64, 256) * slope[m, :, 16:80, :]
-            pgc[m, :, 16:80, :] = grad.astype(BF16)
-            start_sides(*edge)
             got_sides(*edge)
 
         @pl.when(sec == 0)
         def _():
+            skip[0].wait_recv()
             down[0].wait_recv()
-            skip[0].wait_recv()
             upstream = down_in[m, :, 16:80, :].astype(F32) + skip_in[m, :, 16:80, :].astype(F32)
             pgc[m, :, 16:80, :] = (upstream * slope[m, :, 16:80, :]).astype(BF16)
             gather_grads(m)
@@ -568,11 +570,17 @@
             @pl.when(sec >= 4)
             def _():
                 skip_out[m] = branch.astype(BF16).reshape(2, 64, 256)
-                skip[0].start()
-
+
+            def start_skip():
                 @pl.when(sec < 7)
                 def _():
                     start_sides(*skip[1:])
+
+                skip[0].start()
+
+            @pl.when(sec == 4)
+            def _():
+                start_skip()
 
             parts = []
             for kd in range(3):
@@ -596,9 +604,18 @@
 
             down[0].start()
 
+            @pl.when(sec > 4)
+            def _():
+                start_skip()
+
         return carry
 
     lax.fori_loop(0, 2, backward, 0)
+
+    @pl.when(sec == 3)
+    def _():
+        for other in (6, 7):
+            pl.semaphore_signal(token, inc=1, device_id=(other, me), device_id_type=MESH)
 
     @pl.when(sec > 0)
     def _():
@@ -635,27 +652,43 @@
 
     @pl.when(sec >= 6)
     def _():
+        pl.semaphore_wait(token, 1)
         gather_inputs()
 
-    gather_twin(pg.at[0], GRADS)
-    gather_end(pg.at[0], GRADS)
-    spread_grads(pg.at[0], pgs)
-    acc_mix[...] = mix_grad(bt.at[0], pgs)
-
-    def taps(k, carry):
-        kd, kc = k // 3, k % 3
-
-        @pl.when(k == 4)
-        def _():
-            gather_twin(pg.at[1], GRADS + 1)
-
-        found = tap_grads(xt.at[0], pgs, kd, kc)
-        for kr in range(3):
-            acc[kd, kr, kc] = found[kr]
-        return carry
-
-    lax.fori_loop(0, 9, taps, 0)
-    gather_end(pg.at[1], GRADS + 1)
+    half = pl.ds(pl.multiple_of(core * 128, 128), 128)
+    twin = (sec, chip * 2 + 1 - core)
+    for m in range(2):
+        blocks = pgh.at[m, pl.ds(0, 15)]
+        got = remote(blocks, blocks, GRADS + m, (sec, to_left))
+        got.wait_send()
+        got.wait_recv()
+        spread_grads(pgh.at[m], pgs.at[m])
+
+    def both_crops(lhs, kd, rows):
+        found = dot(lhs[0], pgs[0, kd, rows, :]) + dot(lhs[1], pgs[1, kd, rows, :])
+        return found[:256, 128:], found[:256, :128] + found[256:, 128:], found[256:, :128]
+
+    acc_mix[:, half] = both_crops(bt, 1, slice(16, 1040))[1]
+    mixed = remote(acc_mix.at[:, half], acc_mix.at[:, half], MIXED, twin)
+    mixed.start()
+
+    def tap_copy(kd, kc):
+        part = acc.at[kd, :, kc, :, half]
+        return remote(part, part, TAPS, twin)
+
+    for kd in range(3):
+        for kc in range(3):
+            found = both_crops(xt, kd, slice((2 - kc) * 16, (2 - kc) * 16 + 1024))
+            for kr in range(3):
+                acc[kd, kr, kc, :, half] = found[kr]
+            tap_copy(kd, kc).start()
+
+    whole_half = acc.at[:, :, :, :, half]
+    exchanged = remote(whole_half, whole_half, TAPS, twin)
+    mixed.wait_send()
+    mixed.wait_recv()
+    exchanged.wait_send()
+    exchanged.wait_recv()
 
     @pl.when(sec == 7)
     def _():
@@ -711,20 +744,19 @@
     lax.fori_loop(0, 2, finish, 0)
 
 
-def grads_kernel(count, xt, bt, pg, acc, acc_mix, sums, out, out_mix, out_head, out_loss, pgs):
-    kd = pl.program_id(0)
-    kc = pl.program_id(1)
-
-    @pl.when((kd == 0) & (kc == 0))
-    def _():
-        spread_grads(pg.at[1], pgs)
-        out_mix[...] = acc_mix[...] + mix_grad(bt.at[1], pgs)
-        out_head[...] = sums[0:3, :]
-        out_loss[...] = sums[3:4, 0:1] / count
-
-    found = tap_grads(xt.at[1], pgs, kd, kc)
-    for kr in range(3):
-        out[0, kr, 0] = acc[kd, kr, kc] + found[kr]
+def write_kernel(count, acc, acc_mix, sums, out, out_mix, out_head, out_loss, sem):
+    copies = [
+        pltpu.make_async_copy(acc.at[kd, kr], out.at[kd, kr], sem.at[3 * kd + kr])
+        for kd in range(3)
+        for kr in range(3)
+    ]
+    for copy in copies:
+        copy.start()
+    out_mix[...] = acc_mix[...]
+    out_head[...] = sums[0:3, :]
+    out_loss[...] = sums[3:4, 0:1] / count
+    for copy in copies:
+        copy.wait()
 
 
 def body(features_in, labels, offsets, conv_weight, branch_weight, head_weight):
@@ -744,16 +776,17 @@
     middle = pl.pallas_call(
         functools.partial(chain_kernel, count),
         out_shape=(
-            jax.ShapeDtypeStruct((micro, 512, 1024), BF16),
-            jax.ShapeDtypeStruct((micro, 512, 1024), BF16),
-            jax.ShapeDtypeStruct((micro, 2, 8, 2, 64, channels), BF16),
             jax.ShapeDtypeStruct(kernel_shape, F32),
             jax.ShapeDtypeStruct((channels, channels), F32),
             jax.ShapeDtypeStruct((8, channels), F32),
         ),
         in_specs=[hbm] * 6,
-        out_specs=(vmem,) * 6,
+        out_specs=(vmem,) * 3,
         scratch_shapes=[
+            pltpu.VMEM((micro, 512, 1024), BF16),
+            pltpu.VMEM((micro, 512, 1024), BF16),
+            pltpu.VMEM((micro, 2, 2, 64, 128), BF16),
+            pltpu.VMEM((micro, 16, 2, 64, 128), BF16),
             pltpu.VMEM((micro, 128, channels), BF16),
             pltpu.VMEM((micro, rows, columns), jnp.int32),
             pltpu.SMEM((outs, 3), jnp.int32),
@@ -766,12 +799,11 @@
             pltpu.VMEM((16, micro, 16, channels), BF16),
             pltpu.VMEM(gathered, BF16),
             pltpu.VMEM(gathered, BF16),
-            pltpu.VMEM((3, 2, 1056, channels), BF16),
+            pltpu.VMEM((micro, 3, 1056, channels), BF16),
             pltpu.VMEM(wide, BF16),
             pltpu.VMEM(block, BF16),
             pltpu.VMEM(block, BF16),
             pltpu.VMEM(wide, F32),
-            pltpu.VMEM((micro, 128, channels), F32),
             pltpu.VMEM((16, 8, 128), F32),
             pltpu.VMEM((micro, 192, 128), F32),
             pltpu.VMEM(wide, BF16),
@@ -784,6 +816,7 @@
             pltpu.SemaphoreType.DMA((semaphores,)),
             pltpu.SemaphoreType.DMA((semaphores,)),
             pltpu.SemaphoreType.DMA((6,)),
+            pltpu.SemaphoreType.REGULAR,
         ],
         compiler_params=pltpu.CompilerParams(
             collective_id=0, has_side_effects=True, vmem_limit_bytes=34 * 1024 * 1024
@@ -804,23 +837,17 @@
     )
 
     grad_kernel, grad_mixing, grad_head, loss = pl.pallas_call(
-        functools.partial(grads_kernel, count),
-        grid=(3, 3),
+        functools.partial(write_kernel, count),
         out_shape=(
             jax.ShapeDtypeStruct(kernel_shape, F32),
             jax.ShapeDtypeStruct((channels, channels), F32),
             jax.ShapeDtypeStruct((outs, channels), F32),
             jax.ShapeDtypeStruct((1, 1), F32),
         ),
-        in_specs=[vmem] * 6,
-        out_specs=(
-            pl.BlockSpec((1, 3, 1, channels, channels), lambda kd, kc: (kd, 0, kc, 0, 0)),
-            pl.BlockSpec((channels, channels), lambda kd, kc: (0, 0)),
-            pl.BlockSpec((outs, channels), lambda kd, kc: (0, 0)),
-            pl.BlockSpec((1, 1), lambda kd, kc: (0, 0)),
-        ),
-        scratch_shapes=[pltpu.VMEM((3, 2, 1056, channels), BF16)],
-        compiler_params=pltpu.CompilerParams(vmem_limit_bytes=32 * 1024 * 1024),
+        in_specs=[vmem] * 3,
+        out_specs=(hbm, vmem, vmem, vmem),
+        scratch_shapes=[pltpu.SemaphoreType.DMA((9,))],
+        compiler_params=pltpu.CompilerParams(vmem_limit_bytes=16 * 1024 * 1024),
         name="grads",
     )(*middle)
     return (loss.reshape(()), grad_kernel[None], grad_mixing[None], grad_head.T)

time: 134 us -> 133 us (level)
  the two profiles are of different devices: /device:TPU:45 before, /device:TPU:1 now
where the time goes in v3:
time: 133 us; the launch traced here: 132 us
  Pallas kernels  132 us (99%)
    pallas_call x1, Pallas kernels, body(): pl.pallas_call(functools.partial(chain_kernel, count), out_shape=(jax.Sha...  128 us
    pallas_call x1, Pallas kernels, body(): pl.pallas_call(functools.partial(write_kernel, count), out_shape=(jax.Sha...  3.69 us

profile of v3, /device:TPU:1, one launch (start us, length us, event | category | flops | bytes accessed | tf_op | source)
XLA Modules:
  0.0 132.4 jit_solution(5577676116816044293)
XLA Ops:
  0.6 128.1 %chain.1 = (f32[3,3,3,256,256]{4,3,2,1,0:T(8,128)S(1)}, f32[256,256]{1,0:T(8,128)S(1)}, f32[8,256]{1,0:T(8,128)S(1)}) custom-call(bf16[2,128,256]{2,1,0:T(8,128)(2,1)} %bitcast.14, s32[2,2,64]{2,1,0:T(2,128)} %bitcast.16, s32[3,3]{1,0:T(4,128)} %offsets_hbm.1, bf16[3,3,3,256,256]{4,3,2,1,0:T(8,128)(2,1)} %bitcast.13, bf16[256,256]{1,0:T(8,128)(2,1)} %bitcast.15, ...), custom_call_target="tpu_custom_call" | custom-call | tf_op jit(solution)/shard_map/chain/pallas_call | solution.py:776
  128.7 3.7 %grads.1 = (f32[3,3,3,256,256]{4,3,2,1,0:T(8,128)}, f32[256,256]{1,0:T(8,128)}, f32[3,256]{1,0:T(4,128)}, f32[1,1]{1,0:T(1,128)}) custom-call(f32[3,3,3,256,256]{4,3,2,1,0:T(8,128)S(1)} %get-tuple-element.11.acc, f32[256,256]{1,0:T(8,128)S(1)} %get-tuple-element.12.acc_mix, f32[8,256]{1,0:T(8,128)S(1)} %get-tuple-element.13.sums), custom_call_target="tpu_custom_call" | custom-call | tf_op jit(solution)/shard_map/grads/pallas_call | solution.py:839

commit v4 on v3

--- a/solution.py
+++ b/solution.py
@@ -676,13 +676,16 @@
         part = acc.at[kd, :, kc, :, half]
         return remote(part, part, TAPS, twin)
 
-    for kd in range(3):
-        for kc in range(3):
-            found = both_crops(xt, kd, slice((2 - kc) * 16, (2 - kc) * 16 + 1024))
-            for kr in range(3):
-                acc[kd, kr, kc, :, half] = found[kr]
-            tap_copy(kd, kc).start()
-
+    def taps(k, carry):
+        kd, kc = k // 3, k % 3
+        rows = pl.ds(pl.multiple_of((2 - kc) * 16, 16), 1024)
+        found = both_crops(xt, kd, rows)
+        for kr in range(3):
+            acc[kd, kr, kc, :, half] = found[kr]
+        tap_copy(kd, kc).start()
+        return carry
+
+    lax.fori_loop(0, 9, taps, 0)
     whole_half = acc.at[:, :, :, :, half]
     exchanged = remote(whole_half, whole_half, TAPS, twin)
     mixed.wait_send()

time: 133 us -> 128 us (0.962)
  Pallas kernels: 132 us -> 127 us
    pallas_call x1, Pallas kernels: 128 us -> 123 us  [body(): pl.pallas_call(functools.partial(chain_kernel, count), out_shape=(jax.Sha...]
where the time goes in v4:
time: 128 us; the launch traced here: 127 us
  Pallas kernels  127 us (99%)
    pallas_call x1, Pallas kernels, body(): pl.pallas_call(functools.partial(chain_kernel, count), out_shape=(jax.Sha...  123 us
    pallas_call x1, Pallas kernels, body(): pl.pallas_call(functools.partial(write_kernel, count), out_shape=(jax.Sha...  3.69 us

profile of v4, /device:TPU:1, one launch (start us, length us, event | category | flops | bytes accessed | tf_op | source)
XLA Modules:
  0.0 127.4 jit_solution(5919339071350345129)
XLA Ops:
  0.6 123.1 %chain.1 = (f32[3,3,3,256,256]{4,3,2,1,0:T(8,128)S(1)}, f32[256,256]{1,0:T(8,128)S(1)}, f32[8,256]{1,0:T(8,128)S(1)}) custom-call(bf16[2,128,256]{2,1,0:T(8,128)(2,1)} %bitcast.14, s32[2,2,64]{2,1,0:T(2,128)} %bitcast.16, s32[3,3]{1,0:T(4,128)} %offsets_hbm.1, bf16[3,3,3,256,256]{4,3,2,1,0:T(8,128)(2,1)} %bitcast.13, bf16[256,256]{1,0:T(8,128)(2,1)} %bitcast.15, ...), custom_call_target="tpu_custom_call" | custom-call | tf_op jit(solution)/shard_map/chain/pallas_call | solution.py:779
  123.7 3.7 %grads.1 = (f32[3,3,3,256,256]{4,3,2,1,0:T(8,128)}, f32[256,256]{1,0:T(8,128)}, f32[3,256]{1,0:T(4,128)}, f32[1,1]{1,0:T(1,128)}) custom-call(f32[3,3,3,256,256]{4,3,2,1,0:T(8,128)S(1)} %get-tuple-element.11.acc, f32[256,256]{1,0:T(8,128)S(1)} %get-tuple-element.12.acc_mix, f32[8,256]{1,0:T(8,128)S(1)} %get-tuple-element.13.sums), custom_call_target="tpu_custom_call" | custom-call | tf_op jit(solution)/shard_map/grads/pallas_call | solution.py:842

commit v5 on v4

--- a/solution.py
+++ b/solution.py
@@ -14,8 +14,8 @@
 
 
 STAGE, LABELS, HEADS, SUMS, INPUTS, BRANCHES, GRADS, TWIN = 0, 1, 2, 3, 4, 5, 6, 4
-TAPS, MIXED = 10, 11
-BASE, STRIDE = 12, 14
+TAPS, MIXED, STAGE_NEXT = 10, 11, 12
+BASE, STRIDE = 13, 14
 MAIN, MIRROR, SLOPE, DOWN, SKIP, EDGE = 0, 3, 4, 6, 9, 12
 GREETED = 28
 
@@ -218,8 +218,9 @@
         def _():
             right.wait_recv()
 
-    def stage_copy(peer):
-        return remote(pay.at[peer], stage.at[me], STAGE, (sec, peer))
+    def stage_copy(m, peer):
+        index = STAGE_NEXT if m else STAGE
+        return remote(pay.at[peer, m], stage.at[me, m], index, (sec, peer))
 
     def label_copy(peer):
         return remote(laball.at[me], laball.at[me], LABELS, (sec, peer))
@@ -267,11 +268,13 @@
 
     @pl.when(sec == 0)
     def _():
-        def send(step, carry):
-            stage_copy((me + step) % 16).start()
-            return carry
-
-        lax.fori_loop(1, 16, send, 0)
+        for m in range(2):
+
+            def send(step, carry):
+                stage_copy(m, (me + step) % 16).start()
+                return carry
+
+            lax.fori_loop(1, 16, send, 0)
 
     @pl.when(sec == 7)
     def _():
@@ -295,20 +298,6 @@
     @pl.when(sec >= 1)
     def _():
         turn_weights()
-
-    @pl.when(sec == 0)
-    def _():
-        all_staged = remote(stage.at[pl.ds(0, 15)], stage.at[pl.ds(0, 15)], STAGE, (sec, to_left))
-        all_staged.wait_recv()
-        out_row = lax.broadcasted_iota(jnp.int32, (192, 256), 0)
-        in_row = lax.broadcasted_iota(jnp.int32, (192, 256), 1)
-        second = (out_row >= 96).astype(jnp.int32)
-        rest = out_row - 96 * second
-        wanted = (rest & 15) * 16 + second * 8 + (rest >> 4) + 1
-        pick = jnp.where(in_row == wanted, 1.0, 0.0).astype(BF16)
-        for m in range(2):
-            xc[m] = dot(pick, stage[:, m].reshape(256, 256)).astype(BF16).reshape(2, 96, 256)
-        all_staged.wait_send()
 
     @pl.when(sec == 7)
     def _():
@@ -410,8 +399,26 @@
         def _():
             heads[me] = heads[me] + partial
 
+    def place_features(m):
+        index = jnp.where(m > 0, STAGE_NEXT, STAGE)
+        blocks = stage.at[pl.ds(0, 15), m]
+        staged = remote(blocks, blocks, index, (sec, to_left))
+        staged.wait_send()
+        staged.wait_recv()
+        out_row = lax.broadcasted_iota(jnp.int32, (192, 256), 0)
+        in_row = lax.broadcasted_iota(jnp.int32, (192, 256), 1)
+        second = (out_row >= 96).astype(jnp.int32)
+        rest = out_row - 96 * second
+        wanted = (rest & 15) * 16 + second * 8 + (rest >> 4) + 1
+        pick = jnp.where(in_row == wanted, 1.0, 0.0).astype(BF16)
+        xc[m] = dot(pick, stage[:, m].reshape(256, 256)).astype(BF16).reshape(2, 96, 256)
+
     def forward(m, carry):
         main, left, right, mirror = forward_copies(m)
+
+        @pl.when(sec == 0)
+        def _():
+            place_features(m)
 
         @pl.when(sec > 0)
         def _():
@@ -668,9 +675,7 @@
         found = dot(lhs[0], pgs[0, kd, rows, :]) + dot(lhs[1], pgs[1, kd, rows, :])
         return found[:256, 128:], found[:256, :128] + found[256:, 128:], found[256:, :128]
 
-    acc_mix[:, half] = both_crops(bt, 1, slice(16, 1040))[1]
     mixed = remote(acc_mix.at[:, half], acc_mix.at[:, half], MIXED, twin)
-    mixed.start()
 
     def tap_copy(kd, kc):
         part = acc.at[kd, :, kc, :, half]
@@ -686,6 +691,8 @@
         return carry
 
     lax.fori_loop(0, 9, taps, 0)
+    acc_mix[:, half] = both_crops(bt, 1, slice(16, 1040))[1]
+    mixed.start()
     whole_half = acc.at[:, :, :, :, half]
     exchanged = remote(whole_half, whole_half, TAPS, twin)
     mixed.wait_send()

time: 128 us -> 126 us (0.984)
  no operation moved by 1% of the time
where the time goes in v5:
time: 126 us
  Pallas kernels  126 us (100%)
    pallas_call x1, Pallas kernels, body(): pl.pallas_call(functools.partial(chain_kernel, count), out_shape=(jax.Sha...  122 us
    pallas_call x1, Pallas kernels, body(): pl.pallas_call(functools.partial(write_kernel, count), out_shape=(jax.Sha...  3.69 us

profile of v5, /device:TPU:1, one launch (start us, length us, event | category | flops | bytes accessed | tf_op | source)
XLA Modules:
  0.0 126.1 jit_solution(7258798125539728450)
XLA Ops:
  0.6 121.8 %chain.1 = (f32[3,3,3,256,256]{4,3,2,1,0:T(8,128)S(1)}, f32[256,256]{1,0:T(8,128)S(1)}, f32[8,256]{1,0:T(8,128)S(1)}) custom-call(bf16[2,128,256]{2,1,0:T(8,128)(2,1)} %bitcast.14, s32[2,2,64]{2,1,0:T(2,128)} %bitcast.16, s32[3,3]{1,0:T(4,128)} %offsets_hbm.1, bf16[3,3,3,256,256]{4,3,2,1,0:T(8,128)(2,1)} %bitcast.13, bf16[256,256]{1,0:T(8,128)(2,1)} %bitcast.15, ...), custom_call_target="tpu_custom_call" | custom-call | tf_op jit(solution)/shard_map/chain/pallas_call | solution.py:786
  122.4 3.7 %grads.1 = (f32[3,3,3,256,256]{4,3,2,1,0:T(8,128)}, f32[256,256]{1,0:T(8,128)}, f32[3,256]{1,0:T(4,128)}, f32[1,1]{1,0:T(1,128)}) custom-call(f32[3,3,3,256,256]{4,3,2,1,0:T(8,128)S(1)} %get-tuple-element.11.acc, f32[256,256]{1,0:T(8,128)S(1)} %get-tuple-element.12.acc_mix, f32[8,256]{1,0:T(8,128)S(1)} %get-tuple-element.13.sums), custom_call_target="tpu_custom_call" | custom-call | tf_op jit(solution)/shard_map/grads/pallas_call | solution.py:849

commit v6 on v5

--- a/solution.py
+++ b/solution.py
@@ -425,10 +425,6 @@
             main.wait_recv()
             got_sides(left, right)
 
-        @pl.when(sec <= 4)
-        def _():
-            bc[m] = xc[m, :, 16:80, :]
-
         parts = []
         for kd in range(3):
             same = top = bottom = None
@@ -443,7 +439,8 @@
             parts.append(same + jnp.concatenate([top, bottom], axis=0))
 
         preact = parts[1] + shifted(parts[0], -1) + shifted(parts[2], 1)
-        preact = preact + dot(bc[m].reshape(128, 256), mixing[...])
+        branch = jnp.where(sec <= 4, xc[m, :, 16:80, :], bc[m])
+        preact = preact + dot(branch.reshape(128, 256), mixing[...])
         sigma = logistic(preact)
         output = (preact / (1.0 + jnp.exp(-preact))).astype(BF16)
         ys[m] = output.reshape(2, 64, 256)
@@ -535,7 +532,7 @@
         pgo[m, 1] = high
 
         def send(step, carry):
-            grad_copy(m, (me + step) % 16).start()
+            grad_copy(m, (me + 16 - step) % 16).start()
             return carry
 
         lax.fori_loop(1, 16, send, 0)
@@ -554,7 +551,6 @@
             down[0].wait_recv()
             upstream = down_in[m, :, 16:80, :].astype(F32) + skip_in[m, :, 16:80, :].astype(F32)
             pgc[m, :, 16:80, :] = (upstream * slope[m, :, 16:80, :]).astype(BF16)
-            gather_grads(m)
 
         @pl.when((sec > 0) & (sec < 7))
         def _():
@@ -615,6 +611,10 @@
             def _():
                 start_skip()
 
+        @pl.when(sec < 2)
+        def _():
+            gather_grads(m)
+
         return carry
 
     lax.fori_loop(0, 2, backward, 0)
@@ -624,7 +624,7 @@
         for other in (6, 7):
             pl.semaphore_signal(token, inc=1, device_id=(other, me), device_id_type=MESH)
 
-    @pl.when(sec > 0)
+    @pl.when(sec > 1)
     def _():
         for m in range(2):
             gather_grads(m)

time: 126 us -> 126 us (level)
  no operation moved by 1% of the time
where the time goes in v6:
time: 126 us
  Pallas kernels  125 us (99%)
    pallas_call x1, Pallas kernels, body(): pl.pallas_call(functools.partial(chain_kernel, count), out_shape=(jax.Sha...  121 us
    pallas_call x1, Pallas kernels, body(): pl.pallas_call(functools.partial(write_kernel, count), out_shape=(jax.Sha...  3.69 us

profile of v6, /device:TPU:1, one launch (start us, length us, event | category | flops | bytes accessed | tf_op | source)
XLA Modules:
  0.0 125.8 jit_solution(4213007778742413713)
XLA Ops:
  0.6 121.5 %chain.1 = (f32[3,3,3,256,256]{4,3,2,1,0:T(8,128)S(1)}, f32[256,256]{1,0:T(8,128)S(1)}, f32[8,256]{1,0:T(8,128)S(1)}) custom-call(bf16[2,128,256]{2,1,0:T(8,128)(2,1)} %bitcast.14, s32[2,2,64]{2,1,0:T(2,128)} %bitcast.16, s32[3,3]{1,0:T(4,128)} %offsets_hbm.1, bf16[3,3,3,256,256]{4,3,2,1,0:T(8,128)(2,1)} %bitcast.13, bf16[256,256]{1,0:T(8,128)(2,1)} %bitcast.15, ...), custom_call_target="tpu_custom_call" | custom-call | tf_op jit(solution)/shard_map/chain/pallas_call | solution.py:786
  122.1 3.7 %grads.1 = (f32[3,3,3,256,256]{4,3,2,1,0:T(8,128)}, f32[256,256]{1,0:T(8,128)}, f32[3,256]{1,0:T(4,128)}, f32[1,1]{1,0:T(1,128)}) custom-call(f32[3,3,3,256,256]{4,3,2,1,0:T(8,128)S(1)} %get-tuple-element.11.acc, f32[256,256]{1,0:T(8,128)S(1)} %get-tuple-element.12.acc_mix, f32[8,256]{1,0:T(8,128)S(1)} %get-tuple-element.13.sums), custom_call_target="tpu_custom_call" | custom-call | tf_op jit(solution)/shard_map/grads/pallas_call | solution.py:849

commit v7 on v6

--- a/solution.py
+++ b/solution.py
@@ -91,7 +91,7 @@
     ys,
     slope,
     laball,
-    labs,
+    targets,
     down_in,
     down_out,
     skip_in,
@@ -299,54 +299,7 @@
     def _():
         turn_weights()
 
-    @pl.when(sec == 7)
-    def _():
-        labeled = remote(laball.at[pl.ds(0, 15)], laball.at[pl.ds(0, 15)], LABELS, (sec, to_left))
-        labeled.wait_send()
-        labeled.wait_recv()
-        known = laball[...].reshape(128, 128).astype(BF16)
-        out_row = lax.broadcasted_iota(jnp.int32, (192, 128), 0)
-        lane = lax.broadcasted_iota(jnp.int32, (192, 128), 1)
-        second = (out_row >= 96).astype(jnp.int32)
-        rest = out_row - 96 * second
-        for m in range(2):
-            pick = jnp.where(lane == (rest & 15) * 8 + 2 * m + second, 1.0, 0.0).astype(BF16)
-            row = dot(pick, known)
-            here = jnp.where(lane == 4 * me - 1 + (rest >> 4), row, 0.0)
-            labs[m] = jnp.broadcast_to(jnp.sum(here, axis=1, keepdims=True), (192, 128))
-
-    def gather(out, index):
-        def to_peer(peer):
-            block = out.at[core, chip]
-            return remote(block, block, index, (sec, peer * 2 + core))
-
-        def send(step, carry):
-            to_peer((chip + step) % 8).start()
-            return carry
-
-        lax.fori_loop(1, 8, send, 0)
-
-    def gather_twin(out, index):
-        seven = out.at[core, pl.ds(0, 7)]
-        peers = remote(seven, seven, index, (sec, (chip + 1) % 8 * 2 + core))
-        peers.wait_send()
-        peers.wait_recv()
-        remote(out.at[core], out.at[core], index + TWIN, (sec, chip * 2 + 1 - core)).start()
-
-    def gather_end(out, index):
-        twin = remote(out.at[core], out.at[core], index + TWIN, (sec, chip * 2 + 1 - core))
-        twin.wait_send()
-        twin.wait_recv()
-
-    def forward_copies(m):
-        base = BASE + STRIDE * m
-        main, left, right = with_halos(ys.at[m], xc.at[m], base + MAIN, above, 0)
-        mirror = remote(ys.at[m], bc.at[m], base + MIRROR, (7 - sec, me))
-        return main, left, right, mirror
-
-    def loss_and_cotangent(m, output):
-        logits = dot_nt(output, head[...])
-        label = labs[m]
+    def find_targets(label):
         lane = lax.broadcasted_iota(jnp.int32, (1, 128), 1)
 
         def by_channel(k):
@@ -377,7 +330,57 @@
         second = jnp.where(along_row > 0, zero, jnp.where(along_row < 0, rows[0], rows[1]))
         neighbor = jnp.concatenate([first, second], axis=0)
         own = jnp.concatenate([label[16:80], label[112:176]], axis=0)
-        target = jnp.where((neighbor == own) & (own != 0.0), 1.0, 0.0)
+        return jnp.where((neighbor == own) & (own != 0.0), 1.0, 0.0)
+
+    @pl.when(sec == 7)
+    def _():
+        labeled = remote(laball.at[pl.ds(0, 15)], laball.at[pl.ds(0, 15)], LABELS, (sec, to_left))
+        labeled.wait_send()
+        labeled.wait_recv()
+        known = laball[...].reshape(128, 128).astype(BF16)
+        out_row = lax.broadcasted_iota(jnp.int32, (192, 128), 0)
+        lane = lax.broadcasted_iota(jnp.int32, (192, 128), 1)
+        second = (out_row >= 96).astype(jnp.int32)
+        rest = out_row - 96 * second
+        for m in range(2):
+            pick = jnp.where(lane == (rest & 15) * 8 + 2 * m + second, 1.0, 0.0).astype(BF16)
+            row = dot(pick, known)
+            here = jnp.where(lane == 4 * me - 1 + (rest >> 4), row, 0.0)
+            label = jnp.broadcast_to(jnp.sum(here, axis=1, keepdims=True), (192, 128))
+            targets[m] = find_targets(label)
+
+    def gather(out, index):
+        def to_peer(peer):
+            block = out.at[core, chip]
+            return remote(block, block, index, (sec, peer * 2 + core))
+
+        def send(step, carry):
+            to_peer((chip + step) % 8).start()
+            return carry
+
+        lax.fori_loop(1, 8, send, 0)
+
+    def gather_twin(out, index):
+        seven = out.at[core, pl.ds(0, 7)]
+        peers = remote(seven, seven, index, (sec, (chip + 1) % 8 * 2 + core))
+        peers.wait_send()
+        peers.wait_recv()
+        remote(out.at[core], out.at[core], index + TWIN, (sec, chip * 2 + 1 - core)).start()
+
+    def gather_end(out, index):
+        twin = remote(out.at[core], out.at[core], index + TWIN, (sec, chip * 2 + 1 - core))
+        twin.wait_send()
+        twin.wait_recv()
+
+    def forward_copies(m):
+        base = BASE + STRIDE * m
+        main, left, right = with_halos(ys.at[m], xc.at[m], base + MAIN, above, 0)
+        mirror = remote(ys.at[m], bc.at[m], base + MIRROR, (7 - sec, me))
+        return main, left, right, mirror
+
+    def loss_and_cotangent(m, output):
+        logits = dot_nt(output, head[...])
+        target = targets[m]
         channel = lax.broadcasted_iota(jnp.int32, (128, 128), 1) < 3
         grad = jnp.where(channel, loss_scale * (logistic(logits) - target) / count, 0.0)
         rounded = grad.astype(BF16)
@@ -760,9 +763,9 @@
         for kd in range(3)
         for kr in range(3)
     ]
+    copies.append(pltpu.make_async_copy(acc_mix, out_mix, sem.at[9]))
     for copy in copies:
         copy.start()
-    out_mix[...] = acc_mix[...]
     out_head[...] = sums[0:3, :]
     out_loss[...] = sums[3:4, 0:1] / count
     for copy in copies:
@@ -815,7 +818,7 @@
             pltpu.VMEM(block, BF16),
             pltpu.VMEM(wide, F32),
             pltpu.VMEM((16, 8, 128), F32),
-            pltpu.VMEM((micro, 192, 128), F32),
+            pltpu.VMEM((micro, 128, 128), F32),
             pltpu.VMEM(wide, BF16),
             pltpu.VMEM(block, BF16),
             pltpu.VMEM(wide, BF16),
@@ -855,8 +858,8 @@
             jax.ShapeDtypeStruct((1, 1), F32),
         ),
         in_specs=[vmem] * 3,
-        out_specs=(hbm, vmem, vmem, vmem),
-        scratch_shapes=[pltpu.SemaphoreType.DMA((9,))],
+        out_specs=(hbm, hbm, vmem, vmem),
+        scratch_shapes=[pltpu.SemaphoreType.DMA((10,))],
         compiler_params=pltpu.CompilerParams(vmem_limit_bytes=16 * 1024 * 1024),
         name="grads",
     )(*middle)

time: 126 us -> 126 us (level)
  no operation moved by 1% of the time
where the time goes in v7:
time: 126 us
  Pallas kernels  125 us (99%)
    pallas_call x1, Pallas kernels, body(): pl.pallas_call(functools.partial(chain_kernel, count), out_shape=(jax.Sha...  121 us
    pallas_call x1, Pallas kernels, body(): pl.pallas_call(functools.partial(write_kernel, count), out_shape=(jax.Sha...  3.65 us

profile of v7, /device:TPU:1, one launch (start us, length us, event | category | flops | bytes accessed | tf_op | source)
XLA Modules:
  0.0 125.8 jit_solution(16322734023587597685)
XLA Ops:
  0.6 121.5 %chain.1 = (f32[3,3,3,256,256]{4,3,2,1,0:T(8,128)S(1)}, f32[256,256]{1,0:T(8,128)S(1)}, f32[8,256]{1,0:T(8,128)S(1)}) custom-call(bf16[2,128,256]{2,1,0:T(8,128)(2,1)} %bitcast.14, s32[2,2,64]{2,1,0:T(2,128)} %bitcast.16, s32[3,3]{1,0:T(4,128)} %offsets_hbm.1, bf16[3,3,3,256,256]{4,3,2,1,0:T(8,128)(2,1)} %bitcast.13, bf16[256,256]{1,0:T(8,128)(2,1)} %bitcast.15, ...), custom_call_target="tpu_custom_call" | custom-call | tf_op jit(solution)/shard_map/chain/pallas_call | solution.py:789
  122.1 3.6 %grads.1 = (f32[3,3,3,256,256]{4,3,2,1,0:T(8,128)}, f32[256,256]{1,0:T(8,128)}, f32[3,256]{1,0:T(4,128)}, f32[1,1]{1,0:T(1,128)}) custom-call(f32[3,3,3,256,256]{4,3,2,1,0:T(8,128)S(1)} %get-tuple-element.11.acc, f32[256,256]{1,0:T(8,128)S(1)} %get-tuple-element.12.acc_mix, f32[8,256]{1,0:T(8,128)S(1)} %get-tuple-element.13.sums), custom_call_target="tpu_custom_call" | custom-call | tf_op jit(solution)/shard_map/grads/pallas_call | solution.py:852
